TPU v7x, 32 devices: a whole 2x2x4 slice. The times are simulated.
32 devices in a mesh: chan: 8 (over y, x, core), tm: 4 (over z).
Axes of the slice: x: 2, y: 2, z: 4, core: 2. Of those that a mesh axis runs over, the one named last changes fastest.
Arguments:
- records: bfloat16 [128, 16384], P('chan', 'tm'), may hold values from -100 to 100, as said below
- pair_rows: int32 [8, 16], P('chan'), may hold values from 0 to 15, each once within a row
- fir_taps: float32 [32], replicated, may hold values from -1 to 1
- source_blocks: int32 [2], replicated, may hold values from 0 to 15
Outputs:
- stacks: float32 [2, 8, 128, 1024], P(None, None, 'chan', 'tm')
Inputs may be any that keep to these rules, and one draw needn't show every extreme that they name: Seismic noise records, one row a channel.
All inputs are finite; a program needn't handle non-finite values.
Results may differ from a plain program's by a relative error of at most 0.0037.
Values may be sent and summed in bfloat16 or wider, within the bound.
A program may use at most 128 MiB of HBM per device.

v0:
```python
import functools
import math

import jax
import jax.numpy as jnp
from jax import lax
from jax.experimental import pallas as pl
from jax.experimental.pallas import tpu as pltpu
from jax.sharding import PartitionSpec as P

VS = 8
STEPS = 2
LAGS = 1024
TAPS = 32
LANES = 128
FINE = 16


def body(C, T, rows, taps_hbm, pair_hbm, blocks_hbm, rec_hbm, out_ref,
         taps_ref, pair_ref, blocks_ref, rec_ref, local_s,
         halo, phalo, praw, pw, chw, tw, ts, wp, wall,
         halo_s, halo_r, phalo_s, phalo_r, part_s, part_r, pw_s, pw_r, ch_s, ch_r, tw_s, tw_r, ts_s, ts_r):
    me = lax.axis_index("chan")
    t = lax.axis_index("tm")
    f32, bf16 = jnp.float32, jnp.bfloat16
    samples = rec_ref.shape[1] // 4
    lag_dev = LAGS // T
    P_ = max(1, lag_dev // LANES)
    A_ = min(lag_dev, LANES) // FINE
    window = samples * T

    def at_chan(d):
        return lax.rem(me + d, C)

    def at_tm(d):
        return lax.rem(t + d, T)

    loads = [pltpu.make_async_copy(src, dst, local_s.at[i]) for i, (src, dst) in enumerate((
        (taps_hbm, taps_ref), (rec_hbm, rec_ref), (pair_hbm, pair_ref), (blocks_hbm, blocks_ref)))]
    for load in loads:
        load.start()
    barrier = pltpu.get_barrier_semaphore()
    for d in range(1, C):
        pl.semaphore_signal(barrier, inc=1, device_id={"chan": at_chan(d)}, device_id_type=pl.DeviceIdType.MESH)
    for d in range(1, T):
        pl.semaphore_signal(barrier, inc=1, device_id={"tm": at_tm(d)}, device_id_type=pl.DeviceIdType.MESH)

    pl.semaphore_signal(barrier, inc=1, device_id={"chan": at_chan(C // 2), "tm": at_tm(T - 1)},
                        device_id_type=pl.DeviceIdType.MESH)

    def remote(src, dst, ssem, rsem, where):
        return pltpu.make_async_remote_copy(
            src_ref=src, dst_ref=dst, send_sem=ssem, recv_sem=rsem,
            device_id=where, device_id_type=pl.DeviceIdType.MESH)

    group = 4 * LANES
    depth = LANES + group
    j = lax.broadcasted_iota(jnp.int32, (depth, LANES), 0)
    n = lax.broadcasted_iota(jnp.int32, (depth, LANES), 1)
    tap = 4 * n + 3 - (j - LANES)
    band = jnp.zeros((depth, LANES), f32)
    loads[0].wait()
    for k in range(TAPS):
        band = jnp.where(tap == k, taps_ref[k], band)
    hi = band.astype(bf16)
    lo = (band - hi.astype(f32)).astype(bf16)
    band2 = jnp.concatenate([hi, lo], axis=1)

    for load in loads[1:]:
        load.wait()
    pl.semaphore_wait(barrier, C + T - 1)
    tail = rec_ref.shape[1] - LANES
    last = rec_ref.at[:, pl.ds(tail, LANES)]
    phalo_copy = remote(last, phalo, phalo_s, phalo_r, {"chan": at_chan(C // 2), "tm": at_tm(1)})
    halo_copy = remote(last, halo, halo_s, halo_r, {"tm": at_tm(1)})
    part_copy = remote(rec_ref, praw, part_s, part_r, {"chan": at_chan(C // 2)})
    phalo_copy.start()
    halo_copy.start()
    part_copy.start()

    wp[:, window:] = jnp.zeros((rows, wp.shape[1] - window), f32)
    wall[:, window:] = jnp.zeros((wall.shape[0], LANES), bf16)
    rr = lax.broadcasted_iota(jnp.int32, (rows, rows), 0)
    cc = lax.broadcasted_iota(jnp.int32, (rows, rows), 1)
    pick = jnp.zeros((rows, rows), jnp.int32)
    for r in range(rows):
        pick = jnp.where(rr == r, pair_ref[0, r], pick)
    perm = jnp.where(pick == cc, 1.0, 0.0).astype(bf16)

    groups = samples // LANES

    def filter_rows(raw):
        parts = []
        for g in range(groups):
            if g == 0:
                first = jnp.zeros((rows, LANES), bf16)
            else:
                first = raw[:, group * g - LANES:group * g]
            parts.append(jnp.concatenate([first, raw[:, group * g:group * (g + 1)]], axis=1))
        both = jnp.dot(jnp.concatenate(parts, axis=0), band2, preferred_element_type=f32)
        return both[:, :LANES] + both[:, LANES:]

    def permuted(x):
        return jnp.dot(perm, x, preferred_element_type=f32).astype(bf16)

    own = filter_rows(rec_ref[...])
    phalo_copy.wait()
    halo_copy.wait()
    edges = jnp.concatenate([halo[...], permuted(phalo[...])], axis=0)
    edges = jnp.dot(edges, band2[:LANES], preferred_element_type=f32)
    edges = edges[:, :LANES] + edges[:, LANES:]
    edge = edges[:rows] + edges[rows:]
    edge = jnp.where(t > 0, edge, jnp.zeros_like(edge))
    part_copy.wait()
    res = own + filter_rows(permuted(praw[...]))
    filtered = 0.5 * jnp.concatenate(
        [res[:rows] + edge] + [res[rows * g:rows * (g + 1)] for g in range(1, groups)], axis=1)
    sq = filtered * filtered
    acc = sq[:, :LANES]
    for g in range(1, groups):
        acc = acc + sq[:, LANES * g:LANES * (g + 1)]
    pw[t] = acc

    def spread(buf, slot, ssem, rsem, count, axis, place):
        sends = [remote(buf.at[slot], buf.at[slot], ssem.at[d], rsem.at[d], {axis: place(d)})
                 for d in range(1, count)]
        for s in sends:
            s.start()
        return sends

    def arrive(buf, ssem, rsem, count, axis, place):
        for d in range(1, count):
            slot = place(count - d)
            remote(buf.at[slot], buf.at[slot], ssem.at[d], rsem.at[d], {axis: place(d)}).wait_recv()

    pw_sends = spread(pw, t, pw_s, pw_r, T, "tm", at_tm)
    arrive(pw, pw_s, pw_r, T, "tm", at_tm)
    total = pw[0]
    for i in range(1, T):
        total = total + pw[i]
    power = jnp.sum(total, axis=1, keepdims=True) / window
    white = (filtered * lax.rsqrt(power + 1e-6)).astype(bf16)
    chw[me] = white
    tw[t] = white
    ch_sends = spread(chw, me, ch_s, ch_r, C, "chan", at_chan)
    tw_sends = spread(tw, t, tw_s, tw_r, T, "tm", at_tm)

    arrive(chw, ch_s, ch_r, C, "chan", at_chan)
    picked = []
    per = rows // VS
    for step in range(STEPS):
        blk = blocks_ref[step]
        owner = lax.div(blk, per)
        within = lax.rem(blk, per)
        x = chw[owner].astype(f32)
        half = x[:VS]
        for q in range(1, per):
            half = jnp.where(within == q, x[VS * q:VS * (q + 1)], half)
        picked.append(half)
    ts[t] = jnp.concatenate(picked, axis=0).astype(bf16)
    ts_sends = spread(ts, t, ts_s, ts_r, T, "tm", at_tm)
    arrive(tw, tw_s, tw_r, T, "tm", at_tm)
    for i in range(T):
        wp[:, samples * i:samples * (i + 1)] = tw[i].astype(f32)

    lag0 = t * lag_dev
    wide = samples + LANES * P_
    if lag_dev % LANES == 0:
        base, rest = lag0, 0
    else:
        base = lax.div(lag0, LANES) * LANES
        rest = lax.rem(lag0, LANES)

    for i in range(T):
        wrows = wp[:, pl.ds(pl.multiple_of(i * samples + base, LANES), wide)]
        for a in range(A_):
            rolled = wrows
            if lag_dev % LANES:
                rolled = pltpu.roll(wrows, wide - FINE * a - rest, 1)
            elif a:
                rolled = pltpu.roll(wrows, wide - FINE * a, 1)
            for p in range(P_):
                r0 = (p * A_ + a) * rows
                wall[r0:r0 + rows, samples * i:samples * (i + 1)] = (
                    rolled[:, LANES * p:LANES * p + samples].astype(bf16))

    span = samples + LANES

    def term(slot):
        srows = jnp.concatenate([ts[slot].astype(f32), jnp.zeros((rows, LANES), f32)], axis=1)
        xs = []
        for s in range(STEPS * VS):
            one = jnp.broadcast_to(srows[s:s + 1], (FINE, span))
            xs.append(pltpu.roll(one, 0, 1, stride=1, stride_axis=0).astype(bf16))
        ws = wall[:, pl.ds(pl.multiple_of(slot * samples, LANES), span)]
        return lax.dot_general(ws, jnp.concatenate(xs, axis=0),
                               (((1,), (1,)), ((), ())), preferred_element_type=f32)

    z = term(t)
    low = t < T // 2
    edge_dist = jnp.where(low, t, T - 1 - t)
    for k in range(T - 1):
        up = jnp.where(k >= edge_dist, k + 1, k)
        slot = jnp.where(low, up, T - 1 - up)
        d = lax.rem(t - slot + T, T)
        remote(ts.at[slot], ts.at[slot], ts_s.at[d], ts_r.at[d], {"tm": at_tm(d)}).wait_recv()
        z = z + term(slot)
    z = z * (1.0 / math.sqrt(window))

    lane_group = lax.broadcasted_iota(jnp.int32, (rows, LANES), 1) // FINE
    per_tile = LANES // FINE
    width = min(lag_dev, LANES)
    for p in range(P_):
        for lo_s in range(0, STEPS * VS, per_tile):
            turned = []
            for a in range(A_):
                r0 = (p * A_ + a) * rows
                tile = z[r0:r0 + rows, lo_s * FINE:lo_s * FINE + LANES]
                turned.append(pltpu.roll(tile, FINE * a, 1) if a else tile)
            for s in range(per_tile):
                o = turned[0]
                for a in range(1, A_):
                    o = jnp.where(lane_group == (s + a) % per_tile, turned[a], o)
                if s:
                    o = pltpu.roll(o, LANES - FINE * s, 1)
                out_ref[lo_s + s, :, LANES * p:LANES * p + width] = o[:, :width]

    for s in pw_sends + ch_sends + tw_sends + ts_sends:
        s.wait_send()


def shards(records, pair_rows, fir_taps, source_blocks):
    C = lax.axis_size("chan")
    T = lax.axis_size("tm")
    rows, raw = records.shape
    samples = raw // 4
    f32, bf16 = jnp.float32, jnp.bfloat16
    dma = pltpu.SemaphoreType.DMA
    vmem = pl.BlockSpec(memory_space=pltpu.VMEM)
    hbm = pl.BlockSpec(memory_space=pltpu.HBM)
    out = pl.pallas_call(
        functools.partial(body, C, T, rows),
        out_shape=jax.ShapeDtypeStruct((STEPS * VS, rows, LAGS // T), f32),
        in_specs=[hbm] * 4,
        out_specs=vmem,
        scratch_shapes=[
            pltpu.SMEM(fir_taps.shape, f32),
            pltpu.SMEM(pair_rows.shape, jnp.int32),
            pltpu.SMEM(source_blocks.shape, jnp.int32),
            pltpu.VMEM(records.shape, bf16),
            dma((4,)),
            pltpu.VMEM((rows, LANES), bf16),
            pltpu.VMEM((rows, LANES), bf16),
            pltpu.VMEM((rows, raw), bf16),
            pltpu.VMEM((T, rows, LANES), f32),
            pltpu.VMEM((C, rows, samples), bf16),
            pltpu.VMEM((T, rows, samples), bf16),
            pltpu.VMEM((T, rows, samples), bf16),
            pltpu.VMEM((rows, T * samples + LAGS + LANES), f32),
            pltpu.VMEM((LAGS // T // FINE * rows, T * samples + LANES), bf16),
            dma, dma, dma, dma, dma, dma,
            dma((T,)), dma((T,)), dma((C,)), dma((C,)),
            dma((T,)), dma((T,)), dma((T,)), dma((T,)),
        ],
        compiler_params=pltpu.CompilerParams(
            collective_id=0, has_side_effects=True, vmem_limit_bytes=60 * 2**20),
        cost_estimate=pl.CostEstimate(flops=600_000_000, bytes_accessed=1_000_000, transcendentals=0),
    )(fir_taps, pair_rows, source_blocks, records)
    return out.reshape(STEPS, VS, rows, LAGS // T)


def solution(mesh):
    return jax.shard_map(
        shards,
        mesh=mesh,
        in_specs=(P("chan", "tm"), P("chan", None), P(), P()),
        out_specs=P(None, None, "chan", "tm"),
        check_vma=False,
    )
```

profile of v0, /device:TPU:0, one launch (start us, length us, event | category | flops | bytes accessed | tf_op | source)
XLA Modules:
  0.0 26.3 jit_solution(18318130670474948709)
XLA Ops:
  0.0 24.6 %shard_map.46 = f32[16,16,256]{2,1,0:T(8,128)} custom-call(f32[32]{0:T(128)} %taps_hbm.1, s32[1,16]{1,0:T(1,128)} %pair_hbm.1, s32[2]{0:T(128)} %blocks_hbm.1, bf16[16,4096]{1,0:T(8,128)(2,1)} %rec_hbm.1), custom_call_target="tpu_custom_call" | custom-call | flops 600000000 | bytes 1000000 | tf_op jit(solution)/shard_map/pallas_call | solution.py:241
  24.6 1.7 %copy.6 = f32[2,8,16,256]{3,2,1,0:T(8,128)} copy(f32[2,8,16,256]{3,2,1,0:T(8,128)} %bitcast.1) | data formatting | bytes 524288
where the time goes:
time: 26.4 us; the launch traced here: 26.3 us
  Pallas kernels  24.6 us (93%)
  local copies, waits for them, and re-layouts  1.67 us (6%)
    pallas_call x1, Pallas kernels, shards(): pl.pallas_call(functools.partial(body, C, T, rows), out_shape=jax.ShapeDt...  24.6 us
    unnamed x1, local copies, waits for them, and re-layouts  1.67 us

commit v1 on v0

--- a/solution.py
+++ b/solution.py
@@ -55,13 +55,26 @@
 
     group = 4 * LANES
     depth = LANES + group
-    j = lax.broadcasted_iota(jnp.int32, (depth, LANES), 0)
-    n = lax.broadcasted_iota(jnp.int32, (depth, LANES), 1)
-    tap = 4 * n + 3 - (j - LANES)
-    band = jnp.zeros((depth, LANES), f32)
+    row = lax.broadcasted_iota(jnp.int32, (8, LANES), 0)
+    n = lax.broadcasted_iota(jnp.int32, (8, LANES), 1)
+    tap = 4 * n + 3 - row
+    cell = jnp.zeros((8, LANES), f32)
     loads[0].wait()
     for k in range(TAPS):
-        band = jnp.where(tap == k, taps_ref[k], band)
+        cell = jnp.where(tap == k, taps_ref[k], cell)
+    reach = TAPS // 4 + 1
+    tiles = []
+    for b in range(depth // 8):
+        at = 2 * b - LANES // 4
+        tile = jnp.zeros_like(cell)
+        if at > -reach:
+            tile = pltpu.roll(cell, at % LANES, 1) if at else cell
+            if at < 0:
+                tile = jnp.where(n < reach, tile, 0.0)
+            elif at + reach > LANES:
+                tile = jnp.where(n >= reach, tile, 0.0)
+        tiles.append(tile)
+    band = jnp.concatenate(tiles, axis=0)
     hi = band.astype(bf16)
     lo = (band - hi.astype(f32)).astype(bf16)
     band2 = jnp.concatenate([hi, lo], axis=1)
@@ -263,7 +276,7 @@
             dma((T,)), dma((T,)), dma((T,)), dma((T,)),
         ],
         compiler_params=pltpu.CompilerParams(
-            collective_id=0, has_side_effects=True, vmem_limit_bytes=60 * 2**20),
+            collective_id=0, has_side_effects=True, vmem_limit_bytes=(24 if samples * T <= 8192 else 60) * 2**20),
         cost_estimate=pl.CostEstimate(flops=600_000_000, bytes_accessed=1_000_000, transcendentals=0),
     )(fir_taps, pair_rows, source_blocks, records)
     return out.reshape(STEPS, VS, rows, LAGS // T)

time: 26.4 us -> 27.8 us (1.053)
  local copies, waits for them, and re-layouts: 1.67 us -> 3.57 us
  Pallas kernels: 24.6 us -> 24 us
    unnamed x1 -> x9, local copies, waits for them, and re-layouts: 1.67 us -> 3.57 us
    pallas_call x1, Pallas kernels: 24.6 us -> 24 us  [shards(): pl.pallas_call(functools.partial(body, C, T, rows), out_shape=jax.ShapeDt...]
where the time goes in v1:
time: 27.8 us; the launch traced here: 27.6 us
  Pallas kernels  24 us (86%)
  local copies, waits for them, and re-layouts  3.57 us (13%)
    pallas_call x1, Pallas kernels, shards(): pl.pallas_call(functools.partial(body, C, T, rows), out_shape=jax.ShapeDt...  24 us
    unnamed x9, local copies, waits for them, and re-layouts  3.57 us

profile of v1, /device:TPU:0, one launch (start us, length us, event | category | flops | bytes accessed | tf_op | source)
XLA Modules:
  0.0 27.6 jit_solution(4956416230813396373)
XLA Ops:
  0.0 0.0 copy-start
  0.0 0.9 %copy-done = bf16[16,4096]{1,0:T(8,128)(2,1)S(1)} copy-done((bf16[16,4096]{1,0:T(8,128)(2,1)S(1)}, bf16[16,4096]{1,0:T(8,128)(2,1)}, u32[]{:S(2)}) %copy-start) | copy-done | bytes 131096
  0.9 0.0 copy-start.1
  0.9 0.7 %copy-done.1 = f32[32]{0:T(128)S(1)} copy-done((f32[32]{0:T(128)S(1)}, f32[32]{0:T(128)}, u32[]{:S(2)}) %copy-start.1) | copy-done | bytes 152
  1.6 0.0 copy-start.2
  1.6 0.7 %copy-done.2 = s32[1,16]{1,0:T(1,128)S(1)} copy-done((s32[1,16]{1,0:T(1,128)S(1)}, s32[1,16]{1,0:T(1,128)}, u32[]{:S(2)}) %copy-start.2) | copy-done | bytes 88
  2.2 0.0 copy-start.3
  2.2 0.7 %copy-done.3 = s32[2]{0:T(128)S(1)} copy-done((s32[2]{0:T(128)S(1)}, s32[2]{0:T(128)}, u32[]{:S(2)}) %copy-start.3) | copy-done | bytes 32
  2.9 24.0 %shard_map.46 = f32[16,16,256]{2,1,0:T(8,128)S(1)} custom-call(f32[32]{0:T(128)S(1)} %copy-done.1, s32[1,16]{1,0:T(1,128)S(1)} %copy-done.2, s32[2]{0:T(128)S(1)} %copy-done.3, bf16[16,4096]{1,0:T(8,128)(2,1)S(1)} %copy-done), custom_call_target="tpu_custom_call" | custom-call | flops 600000000 | bytes 1000000 | tf_op jit(solution)/shard_map/pallas_call | solution.py:254
  26.9 0.7 %copy.6 = f32[2,8,16,256]{3,2,1,0:T(8,128)} copy(f32[2,8,16,256]{3,2,1,0:T(8,128)S(1)} %bitcast.1) | data formatting | bytes 524288
Async XLA Ops:
  0.0 0.9 %copy-start = (bf16[16,4096]{1,0:T(8,128)(2,1)S(1)}, bf16[16,4096]{1,0:T(8,128)(2,1)}, u32[]{:S(2)}) copy-start(bf16[16,4096]{1,0:T(8,128)(2,1)} %rec_hbm.1) | copy-start | bytes 393220
  0.9 0.7 %copy-start.1 = (f32[32]{0:T(128)S(1)}, f32[32]{0:T(128)}, u32[]{:S(2)}) copy-start(f32[32]{0:T(128)} %taps_hbm.1) | copy-start | bytes 388
  1.6 0.7 %copy-start.2 = (s32[1,16]{1,0:T(1,128)S(1)}, s32[1,16]{1,0:T(1,128)}, u32[]{:S(2)}) copy-start(s32[1,16]{1,0:T(1,128)} %pair_hbm.1) | copy-start | bytes 196
  2.2 0.7 %copy-start.3 = (s32[2]{0:T(128)S(1)}, s32[2]{0:T(128)}, u32[]{:S(2)}) copy-start(s32[2]{0:T(128)} %blocks_hbm.1) | copy-start | bytes 28

commit v2 on v1

--- a/solution.py
+++ b/solution.py
@@ -253,7 +253,7 @@
     hbm = pl.BlockSpec(memory_space=pltpu.HBM)
     out = pl.pallas_call(
         functools.partial(body, C, T, rows),
-        out_shape=jax.ShapeDtypeStruct((STEPS * VS, rows, LAGS // T), f32),
+        out_shape=pltpu.VMEM((STEPS * VS, rows, LAGS // T), f32),
         in_specs=[hbm] * 4,
         out_specs=vmem,
         scratch_shapes=[
@@ -278,7 +278,7 @@
         compiler_params=pltpu.CompilerParams(
             collective_id=0, has_side_effects=True, vmem_limit_bytes=(24 if samples * T <= 8192 else 60) * 2**20),
         cost_estimate=pl.CostEstimate(flops=600_000_000, bytes_accessed=1_000_000, transcendentals=0),
-    )(fir_taps, pair_rows, source_blocks, records)
+    )(*(pltpu.with_memory_space_constraint(x, pltpu.HBM) for x in (fir_taps, pair_rows, source_blocks, records)))
     return out.reshape(STEPS, VS, rows, LAGS // T)
 
 

time: 27.8 us -> 24.6 us (0.88)
  local copies, waits for them, and re-layouts: 3.57 us -> 0.71 us
    unnamed x9 -> x1, local copies, waits for them, and re-layouts: 3.57 us -> 0.71 us
where the time goes in v2:
time: 24.6 us; the launch traced here: 24.5 us
  Pallas kernels  23.8 us (97%)
  local copies, waits for them, and re-layouts  0.71 us (3%)
    pallas_call x1, Pallas kernels, shards(): pl.pallas_call(functools.partial(body, C, T, rows), out_shape=pltpu.VMEM(...  23.8 us
    unnamed x1, local copies, waits for them, and re-layouts  0.71 us

profile of v2, /device:TPU:0, one launch (start us, length us, event | category | flops | bytes accessed | tf_op | source)
XLA Modules:
  0.0 24.5 jit_solution(14064826191687343510)
XLA Ops:
  0.0 23.8 %shard_map.46 = f32[16,16,256]{2,1,0:T(8,128)S(1)} custom-call(f32[32]{0:T(128)} %taps_hbm.1, s32[1,16]{1,0:T(1,128)} %pair_hbm.1, s32[2]{0:T(128)} %blocks_hbm.1, bf16[16,4096]{1,0:T(8,128)(2,1)} %rec_hbm.1), custom_call_target="tpu_custom_call" | custom-call | flops 600000000 | bytes 1000000 | tf_op jit(solution)/shard_map/pallas_call | solution.py:254
  23.8 0.7 %copy.6 = f32[2,8,16,256]{3,2,1,0:T(8,128)} copy(f32[2,8,16,256]{3,2,1,0:T(8,128)S(1)} %bitcast.1) | data formatting | bytes 524288

commit v3 on v0

v3 whole, which is shorter than its diff:
```python
import functools
import math

import jax
import jax.numpy as jnp
from jax import lax
from jax.experimental import pallas as pl
from jax.experimental.pallas import tpu as pltpu
from jax.sharding import PartitionSpec as P

VS = 8
STEPS = 2
LAGS = 1024
TAPS = 32
LANES = 128
FINE = 16
SPILL = TAPS // 4
FULL = 15


def body(C, T, rows, taps_hbm, pair_hbm, blocks_hbm, rec_hbm, out_ref,
         taps_ref, pair_ref, blocks_ref, rec_ref, local_s,
         plane, own, partner, ts, wp, wall,
         plane_s, plane_r, own_s, own_r, partner_s, partner_r, ts_s, ts_r):
    me = lax.axis_index("chan")
    t = lax.axis_index("tm")
    f32, bf16, i16, i32 = jnp.float32, jnp.bfloat16, jnp.int16, jnp.int32
    samples = rec_ref.shape[1] // 4
    width = samples + LANES
    lag_dev = LAGS // T
    P_ = max(1, lag_dev // LANES)
    A_ = min(lag_dev, LANES) // FINE
    window = samples * T

    def at_chan(d):
        return lax.rem(me + d, C)

    def at_tm(d):
        return lax.rem(t + d, T)

    def remote(src, dst, ssem, rsem, where):
        return pltpu.make_async_remote_copy(
            src_ref=src, dst_ref=dst, send_sem=ssem, recv_sem=rsem,
            device_id=where, device_id_type=pl.DeviceIdType.MESH)

    with jax.named_scope("greet"):
        loads = [pltpu.make_async_copy(src, dst, local_s.at[i]) for i, (src, dst) in enumerate((
            (taps_hbm, taps_ref), (rec_hbm, rec_ref), (pair_hbm, pair_ref), (blocks_hbm, blocks_ref)))]
        for load in loads:
            load.start()
        barrier = pltpu.get_barrier_semaphore()
        for d in range(1, C):
            pl.semaphore_signal(barrier, inc=1, device_id={"chan": at_chan(d)}, device_id_type=pl.DeviceIdType.MESH)
        for d in range(1, T):
            pl.semaphore_signal(barrier, inc=1, device_id={"tm": at_tm(d)}, device_id_type=pl.DeviceIdType.MESH)

    with jax.named_scope("band"):
        group = 4 * LANES
        depth = LANES + group
        row = lax.broadcasted_iota(i32, (8, LANES), 0)
        n = lax.broadcasted_iota(i32, (8, LANES), 1)
        tap = 4 * n + 3 - row
        cell = jnp.zeros((8, LANES), f32)
        loads[0].wait()
        for k in range(TAPS):
            cell = jnp.where(tap == k, taps_ref[k], cell)
        reach = TAPS // 4 + 1
        tiles = []
        for b in range(depth // 8):
            at = 2 * b - LANES // 4
            tile = jnp.zeros_like(cell)
            if at > -reach:
                tile = pltpu.roll(cell, at % LANES, 1) if at else cell
                if at < 0:
                    tile = jnp.where(n < reach, tile, 0.0)
                elif at + reach > LANES:
                    tile = jnp.where(n >= reach, tile, 0.0)
            tiles.append(tile)
        band = jnp.concatenate(tiles, axis=0)
        hi = band.astype(bf16)
        lo = (band - hi.astype(f32)).astype(bf16)
        band2 = jnp.concatenate([hi, lo], axis=1)
        for load in loads[1:]:
            load.wait()

    groups = samples // LANES
    lane = lax.broadcasted_iota(i32, (rows, LANES), 1)

    def encode(x, note):
        peak = jnp.maximum(jnp.max(jnp.abs(x), axis=1, keepdims=True), 1e-30)
        e = jnp.floor(jnp.log2(peak)) + 1.0
        q = jnp.clip(jnp.round(x * jnp.exp2(FULL - e)), -32767.0, 32767.0).astype(i32)
        last = jnp.where(lane == SPILL, e.astype(i32), jnp.where(lane == SPILL + 1, note, q[:, samples:]))
        return jnp.concatenate([q[:, :samples], last], axis=1).astype(i16)

    def scaled(v):
        return v * jnp.exp2(v[:, samples + SPILL:samples + SPILL + 1] - (FULL + 1))

    def plain(x):
        return x.astype(i32).astype(f32)

    def permuted(onehot, x):
        v = x.astype(i32)
        pair = jnp.concatenate([(v >> 8).astype(f32).astype(bf16), (v & 255).astype(f32).astype(bf16)], axis=1)
        both = jnp.dot(onehot, pair, preferred_element_type=f32)
        return 256.0 * both[:, :width] + both[:, width:]

    with jax.named_scope("filter"):
        raw = rec_ref[...]
        parts = []
        for g in range(groups):
            if g == 0:
                first = jnp.zeros((rows, LANES), bf16)
            else:
                first = raw[:, group * g - LANES:group * g]
            parts.append(jnp.concatenate([first, raw[:, group * g:group * (g + 1)]], axis=1))
        both = jnp.dot(jnp.concatenate(parts, axis=0), band2, preferred_element_type=f32)
        both = both[:, :LANES] + both[:, LANES:]
        edge = jnp.dot(raw[:, group * groups - LANES:], band2[:LANES], preferred_element_type=f32)
        edge = edge[:, :LANES] + edge[:, LANES:]
        filtered = jnp.concatenate([both[rows * g:rows * (g + 1)] for g in range(groups)] + [edge], axis=1)
        rr = lax.broadcasted_iota(i32, (rows, LANES), 0)
        pick = jnp.zeros((rows, LANES), i32)
        for r in range(rows):
            pick = jnp.where(rr == r, pair_ref[0, r], pick)
        perm = jnp.where(pick[:, :rows] == lax.broadcasted_iota(i32, (rows, rows), 1), 1.0, 0.0).astype(bf16)
        code = encode(filtered, pick)
        plane[me] = code
        own[t] = code

    with jax.named_scope("wait_greeting"):
        pl.semaphore_wait(barrier, C + T - 2)

    half = C // 2
    with jax.named_scope("send_filtered"):
        order = [half] + [d for d in range(1, C) if d != half]
        sends = [remote(plane.at[me], plane.at[me], plane_s.at[d], plane_r.at[d], {"chan": at_chan(d)}) for d in order]
        sends += [remote(own.at[t], own.at[t], own_s.at[d], own_r.at[d], {"tm": at_tm(d)}) for d in range(1, T)]
        for s in sends[:1] + sends[C - 1:] + sends[1:C - 1]:
            s.start()

    with jax.named_scope("clear"):
        wp[:, window:] = jnp.zeros((rows, wp.shape[1] - window), f32)
        wall[:, window:] = jnp.zeros((wall.shape[0], LANES), bf16)

    low = t < T // 2
    edge_dist = jnp.where(low, t, T - 1 - t)

    def near(k):
        up = jnp.where(k >= edge_dist, k + 1, k)
        slot = jnp.where(low, up, T - 1 - up)
        return slot, lax.rem(t - slot + T, T)

    relays = []

    def relay(k):
        slot, d = near(k)
        remote(own.at[slot], own.at[slot], own_s.at[d], own_r.at[d], {"tm": at_tm(d)}).wait_recv()
        s = remote(own.at[slot], partner.at[slot], partner_s.at[d], partner_r.at[d], {"chan": at_chan(half)})
        s.start()
        relays.append(s)

    with jax.named_scope("relay_first"):
        relay(0)

    with jax.named_scope("wait_plane"):
        for d in order:
            slot = at_chan(C - d)
            remote(plane.at[slot], plane.at[slot], plane_s.at[d], plane_r.at[d], {"chan": at_chan(d)}).wait_recv()

    with jax.named_scope("pick"):
        picked = []
        per = rows // VS

        def halved(x, within):
            y = x[:VS]
            for q in range(1, per):
                y = jnp.where(within == q, x[VS * q:VS * (q + 1)], y)
            return y

        for step in range(STEPS):
            blk = blocks_ref[step]
            owner = lax.div(blk, per)
            within = lax.rem(blk, per)
            mine = halved(plain(plane[owner]), within)
            pair = mine[:, samples + SPILL + 1:samples + SPILL + 2]
            onehot = jnp.where(pair == lax.broadcasted_iota(i32, (VS, rows), 1).astype(f32), 1.0, 0.0).astype(bf16)
            theirs = permuted(onehot, plane[lax.rem(owner + half, C)])
            picked.append(scaled(mine) + scaled(theirs))
        ts[t] = encode(jnp.concatenate(picked, axis=0), jnp.zeros((rows, LANES), i32))
        ts_sends = [remote(ts.at[t], ts.at[t], ts_s.at[d], ts_r.at[d], {"tm": at_tm(d)}) for d in range(1, T)]
        for s in ts_sends:
            s.start()

    with jax.named_scope("relay_rest"):
        for k in range(1, T - 1):
            relay(k)

    def assemble(blocks):
        out = []
        for i, x in enumerate(blocks):
            head = x[:, :LANES]
            if i:
                head = head + jnp.where(lane < SPILL, blocks[i - 1][:, samples:], 0.0)
            out.append(jnp.concatenate([head, x[:, LANES:samples]], axis=1))
        return out

    def whiten(blocks):
        acc = jnp.zeros((rows, LANES), f32)
        for x in blocks:
            sq = x * x
            for g in range(groups):
                acc = acc + sq[:, LANES * g:LANES * (g + 1)]
        scale = lax.rsqrt(jnp.sum(acc, axis=1, keepdims=True) / window + 1e-6)
        return [(x * scale).astype(bf16) for x in blocks]

    with jax.named_scope("wait_partner"):
        partner[t] = plane[at_chan(half)]
        for k in range(T - 1):
            slot, d = near(k)
            remote(partner.at[slot], partner.at[slot], partner_s.at[d], partner_r.at[d],
                   {"chan": at_chan(half)}).wait_recv()

    with jax.named_scope("white"):
        white = whiten(assemble([scaled(plain(own[i])) + scaled(permuted(perm, partner[i])) for i in range(T)]))
        for i in range(T):
            wp[:, samples * i:samples * (i + 1)] = white[i].astype(f32)

    with jax.named_scope("wall"):
        lag0 = t * lag_dev
        wide = samples + LANES * P_
        if lag_dev % LANES == 0:
            base, rest = lag0, 0
        else:
            base = lax.div(lag0, LANES) * LANES
            rest = lax.rem(lag0, LANES)
        for i in range(T):
            wrows = wp[:, pl.ds(pl.multiple_of(i * samples + base, LANES), wide)]
            for a in range(A_):
                rolled = wrows
                if lag_dev % LANES:
                    rolled = pltpu.roll(wrows, wide - FINE * a - rest, 1)
                elif a:
                    rolled = pltpu.roll(wrows, wide - FINE * a, 1)
                for p in range(P_):
                    r0 = (p * A_ + a) * rows
                    wall[r0:r0 + rows, samples * i:samples * (i + 1)] = (
                        rolled[:, LANES * p:LANES * p + samples].astype(bf16))

    with jax.named_scope("wait_sources"):
        for k in range(T - 1):
            slot, d = near(k)
            remote(ts.at[slot], ts.at[slot], ts_s.at[d], ts_r.at[d], {"tm": at_tm(d)}).wait_recv()

    with jax.named_scope("sources"):
        sources = whiten(assemble([2.0 * scaled(plain(ts[i])) for i in range(T)]))

    span = samples + LANES
    with jax.named_scope("correlate"):
        z = None
        for i in range(T):
            srows = jnp.concatenate([sources[i].astype(f32), jnp.zeros((rows, LANES), f32)], axis=1)
            xs = []
            for s in range(STEPS * VS):
                one = jnp.broadcast_to(srows[s:s + 1], (FINE, span))
                xs.append(pltpu.roll(one, 0, 1, stride=1, stride_axis=0).astype(bf16))
            ws = wall[:, samples * i:samples * i + span]
            term = lax.dot_general(ws, jnp.concatenate(xs, axis=0),
                                   (((1,), (1,)), ((), ())), preferred_element_type=f32)
            z = term if z is None else z + term
        z = z * (1.0 / math.sqrt(window))

    with jax.named_scope("result"):
        lane_group = lane // FINE
        per_tile = LANES // FINE
        span_out = min(lag_dev, LANES)
        for p in range(P_):
            for lo_s in range(0, STEPS * VS, per_tile):
                turned = []
                for a in range(A_):
                    r0 = (p * A_ + a) * rows
                    tile = z[r0:r0 + rows, lo_s * FINE:lo_s * FINE + LANES]
                    turned.append(pltpu.roll(tile, FINE * a, 1) if a else tile)
                for s in range(per_tile):
                    o = turned[0]
                    for a in range(1, A_):
                        o = jnp.where(lane_group == (s + a) % per_tile, turned[a], o)
                    if s:
                        o = pltpu.roll(o, LANES - FINE * s, 1)
                    out_ref[lo_s + s, :, LANES * p:LANES * p + span_out] = o[:, :span_out]

    with jax.named_scope("wait_sends"):
        for s in sends + relays + ts_sends:
            s.wait_send()


def shards(records, pair_rows, fir_taps, source_blocks):
    C = lax.axis_size("chan")
    T = lax.axis_size("tm")
    rows, raw = records.shape
    samples = raw // 4
    f32, bf16, i16 = jnp.float32, jnp.bfloat16, jnp.int16
    dma = pltpu.SemaphoreType.DMA
    hbm = pl.BlockSpec(memory_space=pltpu.HBM)
    operands = [pltpu.with_memory_space_constraint(x, pltpu.HBM)
                for x in (fir_taps, pair_rows, source_blocks, records)]
    out = pl.pallas_call(
        functools.partial(body, C, T, rows),
        out_shape=pltpu.VMEM((STEPS * VS, rows, LAGS // T), f32),
        in_specs=[hbm] * 4,
        out_specs=pl.BlockSpec(memory_space=pltpu.VMEM),
        scratch_shapes=[
            pltpu.SMEM(fir_taps.shape, f32),
            pltpu.SMEM(pair_rows.shape, jnp.int32),
            pltpu.SMEM(source_blocks.shape, jnp.int32),
            pltpu.VMEM(records.shape, bf16),
            dma((4,)),
            pltpu.VMEM((C, rows, samples + LANES), i16),
            pltpu.VMEM((T, rows, samples + LANES), i16),
            pltpu.VMEM((T, rows, samples + LANES), i16),
            pltpu.VMEM((T, rows, samples + LANES), i16),
            pltpu.VMEM((rows, T * samples + LAGS + LANES), f32),
            pltpu.VMEM((LAGS // T // FINE * rows, T * samples + LANES), bf16),
            dma((C,)), dma((C,)), dma((T,)), dma((T,)), dma((T,)), dma((T,)), dma((T,)), dma((T,)),
        ],
        compiler_params=pltpu.CompilerParams(
            collective_id=0, has_side_effects=True,
            vmem_limit_bytes=(24 if samples * T <= 8192 else 60) * 2**20),
        cost_estimate=pl.CostEstimate(flops=600_000_000, bytes_accessed=1_000_000, transcendentals=0),
    )(*operands)
    return out.reshape(STEPS, VS, rows, LAGS // T)


def solution(mesh):
    return jax.shard_map(
        shards,
        mesh=mesh,
        in_specs=(P("chan", "tm"), P("chan", None), P(), P()),
        out_specs=P(None, None, "chan", "tm"),
        check_vma=False,
    )
```

time: 26.4 us -> 18.2 us (0.69)
  Pallas kernels: 24.6 us -> 17.3 us
  local copies, waits for them, and re-layouts: 1.67 us -> 0.71 us
    pallas_call x1, Pallas kernels: 24.6 us -> 17.3 us  [shards(): pl.pallas_call(functools.partial(body, C, T, rows), out_shape=pltpu.VMEM(...]
    unnamed x1, local copies, waits for them, and re-layouts: 1.67 us -> 0.71 us
where the time goes in v3:
time: 18.2 us; the launch traced here: 18 us
  Pallas kernels  17.3 us (95%)
  local copies, waits for them, and re-layouts  0.71 us (4%)
    pallas_call x1, Pallas kernels, shards(): pl.pallas_call(functools.partial(body, C, T, rows), out_shape=pltpu.VMEM(...  17.3 us
    unnamed x1, local copies, waits for them, and re-layouts  0.71 us

profile of v3, /device:TPU:0, one launch (start us, length us, event | category | flops | bytes accessed | tf_op | source)
XLA Modules:
  0.0 18.0 jit_solution(7366585124770596386)
XLA Ops:
  0.0 17.3 %shard_map.46 = f32[16,16,256]{2,1,0:T(8,128)S(1)} custom-call(f32[32]{0:T(128)} %taps_hbm.1, s32[1,16]{1,0:T(1,128)} %pair_hbm.1, s32[2]{0:T(128)} %blocks_hbm.1, bf16[16,4096]{1,0:T(8,128)(2,1)} %rec_hbm.1), custom_call_target="tpu_custom_call" | custom-call | flops 600000000 | bytes 1000000 | tf_op jit(solution)/shard_map/pallas_call | solution.py:307
  17.3 0.7 %copy.6 = f32[2,8,16,256]{3,2,1,0:T(8,128)} copy(f32[2,8,16,256]{3,2,1,0:T(8,128)S(1)} %bitcast.1) | data formatting | bytes 524288

commit v4 on v3

--- a/solution.py
+++ b/solution.py
@@ -20,13 +20,17 @@
 
 def body(C, T, rows, taps_hbm, pair_hbm, blocks_hbm, rec_hbm, out_ref,
          taps_ref, pair_ref, blocks_ref, rec_ref, local_s,
-         plane, own, partner, ts, wp, wall,
-         plane_s, plane_r, own_s, own_r, partner_s, partner_r, ts_s, ts_r):
+         halves, plane, own, partner, small, body_, wp, wall,
+         plane_s, plane_r, own_s, own_r, partner_s, partner_r, small_s, small_r, body_s, body_r, twin_s, twin_r):
     me = lax.axis_index("chan")
     t = lax.axis_index("tm")
     f32, bf16, i16, i32 = jnp.float32, jnp.bfloat16, jnp.int16, jnp.int32
     samples = rec_ref.shape[1] // 4
     width = samples + LANES
+    part = samples // 2
+    half = C // 2
+    side = lax.rem(me, 2)
+    twin = me + 1 - 2 * side
     lag_dev = LAGS // T
     P_ = max(1, lag_dev // LANES)
     A_ = min(lag_dev, LANES) // FINE
@@ -53,6 +57,8 @@
             pl.semaphore_signal(barrier, inc=1, device_id={"chan": at_chan(d)}, device_id_type=pl.DeviceIdType.MESH)
         for d in range(1, T):
             pl.semaphore_signal(barrier, inc=1, device_id={"tm": at_tm(d)}, device_id_type=pl.DeviceIdType.MESH)
+            pl.semaphore_signal(barrier, inc=1, device_id={"chan": twin, "tm": at_tm(d)},
+                                device_id_type=pl.DeviceIdType.MESH)
 
     with jax.named_scope("band"):
         group = 4 * LANES
@@ -86,15 +92,14 @@
     groups = samples // LANES
     lane = lax.broadcasted_iota(i32, (rows, LANES), 1)
 
-    def encode(x, note):
+    def encode(x):
         peak = jnp.maximum(jnp.max(jnp.abs(x), axis=1, keepdims=True), 1e-30)
         e = jnp.floor(jnp.log2(peak)) + 1.0
-        q = jnp.clip(jnp.round(x * jnp.exp2(FULL - e)), -32767.0, 32767.0).astype(i32)
-        last = jnp.where(lane == SPILL, e.astype(i32), jnp.where(lane == SPILL + 1, note, q[:, samples:]))
-        return jnp.concatenate([q[:, :samples], last], axis=1).astype(i16)
+        return jnp.clip(jnp.round(x * jnp.exp2(FULL - e)), -32767.0, 32767.0).astype(i32), e
 
     def scaled(v):
-        return v * jnp.exp2(v[:, samples + SPILL:samples + SPILL + 1] - (FULL + 1))
+        at = v.shape[1] - LANES + SPILL
+        return v * jnp.exp2(v[:, at:at + 1] - (FULL + 1))
 
     def plain(x):
         return x.astype(i32).astype(f32)
@@ -103,7 +108,7 @@
         v = x.astype(i32)
         pair = jnp.concatenate([(v >> 8).astype(f32).astype(bf16), (v & 255).astype(f32).astype(bf16)], axis=1)
         both = jnp.dot(onehot, pair, preferred_element_type=f32)
-        return 256.0 * both[:, :width] + both[:, width:]
+        return 256.0 * both[:, :x.shape[1]] + both[:, x.shape[1]:]
 
     with jax.named_scope("filter"):
         raw = rec_ref[...]
@@ -124,19 +129,24 @@
         for r in range(rows):
             pick = jnp.where(rr == r, pair_ref[0, r], pick)
         perm = jnp.where(pick[:, :rows] == lax.broadcasted_iota(i32, (rows, rows), 1), 1.0, 0.0).astype(bf16)
-        code = encode(filtered, pick)
-        plane[me] = code
-        own[t] = code
+        q, e = encode(filtered)
+        note = jnp.where(lane == SPILL, e.astype(i32), jnp.where(lane == SPILL + 1, pick, q[:, samples:])).astype(i16)
+        q = q[:, :samples].astype(i16)
+        own[t] = jnp.concatenate([q, note], axis=1)
+        halves[0] = jnp.concatenate([q[:, :part], note], axis=1)
+        halves[1] = jnp.concatenate([q[:, part:], note], axis=1)
+        plane[me] = halves[side]
 
     with jax.named_scope("wait_greeting"):
-        pl.semaphore_wait(barrier, C + T - 2)
-
-    half = C // 2
+        pl.semaphore_wait(barrier, C + 2 * T - 3)
+
     with jax.named_scope("send_filtered"):
-        order = [half] + [d for d in range(1, C) if d != half]
-        sends = [remote(plane.at[me], plane.at[me], plane_s.at[d], plane_r.at[d], {"chan": at_chan(d)}) for d in order]
+        others = [d for d in range(1, C) if d != half]
+        sends = [remote(own.at[t], partner.at[t], partner_s.at[0], partner_r.at[0], {"chan": at_chan(half)})]
         sends += [remote(own.at[t], own.at[t], own_s.at[d], own_r.at[d], {"tm": at_tm(d)}) for d in range(1, T)]
-        for s in sends[:1] + sends[C - 1:] + sends[1:C - 1]:
+        sends += [remote(halves.at[lax.rem(side + d, 2)], plane.at[me], plane_s.at[d], plane_r.at[d],
+                         {"chan": at_chan(d)}) for d in others]
+        for s in sends:
             s.start()
 
     with jax.named_scope("clear"):
@@ -164,11 +174,19 @@
         relay(0)
 
     with jax.named_scope("wait_plane"):
-        for d in order:
+        for d in others:
             slot = at_chan(C - d)
-            remote(plane.at[slot], plane.at[slot], plane_s.at[d], plane_r.at[d], {"chan": at_chan(d)}).wait_recv()
+            remote(halves.at[0], plane.at[slot], plane_s.at[d], plane_r.at[d], {"chan": at_chan(d)}).wait_recv()
+        remote(own.at[t], partner.at[t], partner_s.at[0], partner_r.at[0], {"chan": at_chan(half)}).wait_recv()
+
+    with jax.named_scope("relay_rest"):
+        for k in range(1, max(1, T - 2)):
+            relay(k)
 
     with jax.named_scope("pick"):
+        mate = partner[t]
+        body_half = jnp.where(side == 0, plain(mate[:, :part]), plain(mate[:, part:samples]))
+        plane[at_chan(half)] = jnp.concatenate([body_half.astype(i32).astype(i16), mate[:, samples:]], axis=1)
         picked = []
         per = rows // VS
 
@@ -183,17 +201,43 @@
             owner = lax.div(blk, per)
             within = lax.rem(blk, per)
             mine = halved(plain(plane[owner]), within)
-            pair = mine[:, samples + SPILL + 1:samples + SPILL + 2]
+            pair = mine[:, part + SPILL + 1:part + SPILL + 2]
             onehot = jnp.where(pair == lax.broadcasted_iota(i32, (VS, rows), 1).astype(f32), 1.0, 0.0).astype(bf16)
             theirs = permuted(onehot, plane[lax.rem(owner + half, C)])
             picked.append(scaled(mine) + scaled(theirs))
-        ts[t] = encode(jnp.concatenate(picked, axis=0), jnp.zeros((rows, LANES), i32))
-        ts_sends = [remote(ts.at[t], ts.at[t], ts_s.at[d], ts_r.at[d], {"tm": at_tm(d)}) for d in range(1, T)]
+        x = jnp.concatenate(picked, axis=0)
+        q, e = encode(x[:, :part])
+        spill, head = x[:, part:], x[:, :LANES]
+        sq = jnp.where((lane < SPILL) & (side == 0), 0.0, head * head)
+        for g in range(1, part // LANES):
+            y = x[:, LANES * g:LANES * (g + 1)]
+            sq = sq + y * y
+        facts = jnp.where(lane < SPILL, spill, jnp.where(lane < 2 * SPILL, pltpu.roll(head, SPILL, 1), jnp.where(
+            lane == 2 * SPILL, jnp.exp2(e - FULL), jnp.sum(sq, axis=1, keepdims=True))))
+        low_lane = lane[:VS] < LANES // 2
+        mine_at = 2 * t + side
+        small[mine_at] = jnp.where(low_lane, facts[:VS], pltpu.roll(facts[VS:], LANES // 2, 1))
+        body_[mine_at] = q.astype(i16)
+        away = [(d, p) for d in range(T) for p in range(2) if d or p]
+
+        def small_copy(d, p, at):
+            where = {"tm": at_tm(d)} if p == 0 else {"chan": twin, "tm": at_tm(d)}
+            return remote(small.at[at], small.at[at], small_s.at[2 * d + p], small_r.at[2 * d + p], where)
+
+        def twin_copy(d, at):
+            return remote(body_.at[at], body_.at[at], twin_s.at[d], twin_r.at[d], {"chan": twin})
+
+        def body_copy(d, at):
+            return remote(body_.at[at], body_.at[at], body_s.at[d], body_r.at[d], {"tm": at_tm(d)})
+
+        ts_sends = [small_copy(d, p, mine_at) for d, p in away if d]
+        ts_sends += [body_copy(d, mine_at) for d in range(1, T)]
+        ts_sends += [small_copy(0, 1, mine_at), twin_copy(0, mine_at)]
         for s in ts_sends:
             s.start()
 
-    with jax.named_scope("relay_rest"):
-        for k in range(1, T - 1):
+    with jax.named_scope("relay_last"):
+        for k in range(max(1, T - 2), T - 1):
             relay(k)
 
     def assemble(blocks):
@@ -215,7 +259,6 @@
         return [(x * scale).astype(bf16) for x in blocks]
 
     with jax.named_scope("wait_partner"):
-        partner[t] = plane[at_chan(half)]
         for k in range(T - 1):
             slot, d = near(k)
             remote(partner.at[slot], partner.at[slot], partner_s.at[d], partner_r.at[d],
@@ -247,28 +290,64 @@
                     wall[r0:r0 + rows, samples * i:samples * (i + 1)] = (
                         rolled[:, LANES * p:LANES * p + samples].astype(bf16))
 
-    with jax.named_scope("wait_sources"):
+    with jax.named_scope("wait_small"):
+        for d, p in away:
+            from_side = side if p == 0 else 1 - side
+            small_copy(d, p, 2 * at_tm(T - d) + from_side).wait_recv()
+
+    with jax.named_scope("hand_to_twin"):
         for k in range(T - 1):
             slot, d = near(k)
-            remote(ts.at[slot], ts.at[slot], ts_s.at[d], ts_r.at[d], {"tm": at_tm(d)}).wait_recv()
-
-    with jax.named_scope("sources"):
-        sources = whiten(assemble([2.0 * scaled(plain(ts[i])) for i in range(T)]))
+            body_copy(d, 2 * slot + side).wait_recv()
+            s = twin_copy(d, 2 * slot + side)
+            s.start()
+            relays.append(s)
+
+    with jax.named_scope("source_power"):
+        def facts_of(at):
+            x = small[at]
+            return jnp.concatenate([x, pltpu.roll(x, LANES // 2, 1)], axis=0)
+
+        total = jnp.zeros((rows, LANES), f32)
+        before = None
+        for i in range(T):
+            first, second = facts_of(2 * i), facts_of(2 * i + 1)
+            head = pltpu.roll(first, LANES - SPILL, 1)
+            if before is not None:
+                head = head + before
+            before = second
+            total = total + jnp.where(lane < SPILL, head * head, jnp.where(lane == 2 * SPILL + 1, first + second, 0.0))
+        source_scale = lax.rsqrt(jnp.sum(total, axis=1, keepdims=True) / window + 1e-6)
 
     span = samples + LANES
+
+    def term(slot):
+        first, second = facts_of(2 * slot), facts_of(2 * slot + 1)
+        before = jnp.where((slot > 0) & (lane < SPILL), facts_of(2 * jnp.maximum(slot, 1) - 1), 0.0)
+        x = jnp.concatenate([plain(body_[2 * slot]) * first[:, 2 * SPILL:2 * SPILL + 1],
+                             plain(body_[2 * slot + 1]) * second[:, 2 * SPILL:2 * SPILL + 1]], axis=1)
+        x = jnp.concatenate([x[:, :LANES] + before, x[:, LANES:]], axis=1) * source_scale
+        x = x.astype(bf16).astype(f32)
+        srows = jnp.concatenate([x, jnp.zeros((rows, LANES), f32)], axis=1)
+        xs = []
+        for s in range(STEPS * VS):
+            one = jnp.broadcast_to(srows[s:s + 1], (FINE, span))
+            xs.append(pltpu.roll(one, 0, 1, stride=1, stride_axis=0).astype(bf16))
+        ws = wall[:, pl.ds(pl.multiple_of(slot * samples, LANES), span)]
+        return lax.dot_general(ws, jnp.concatenate(xs, axis=0),
+                               (((1,), (1,)), ((), ())), preferred_element_type=f32)
+
+    with jax.named_scope("wait_twin_own"):
+        twin_copy(0, 2 * t + 1 - side).wait_recv()
     with jax.named_scope("correlate"):
-        z = None
-        for i in range(T):
-            srows = jnp.concatenate([sources[i].astype(f32), jnp.zeros((rows, LANES), f32)], axis=1)
-            xs = []
-            for s in range(STEPS * VS):
-                one = jnp.broadcast_to(srows[s:s + 1], (FINE, span))
-                xs.append(pltpu.roll(one, 0, 1, stride=1, stride_axis=0).astype(bf16))
-            ws = wall[:, samples * i:samples * i + span]
-            term = lax.dot_general(ws, jnp.concatenate(xs, axis=0),
-                                   (((1,), (1,)), ((), ())), preferred_element_type=f32)
-            z = term if z is None else z + term
-        z = z * (1.0 / math.sqrt(window))
+        z = term(t)
+    for k in range(T - 1):
+        slot, d = near(k)
+        with jax.named_scope("wait_twin"):
+            twin_copy(d, 2 * slot + 1 - side).wait_recv()
+        with jax.named_scope("correlate"):
+            z = z + term(slot)
+    z = z * (1.0 / math.sqrt(window))
 
     with jax.named_scope("result"):
         lane_group = lane // FINE
@@ -315,13 +394,16 @@
             pltpu.SMEM(source_blocks.shape, jnp.int32),
             pltpu.VMEM(records.shape, bf16),
             dma((4,)),
-            pltpu.VMEM((C, rows, samples + LANES), i16),
+            pltpu.VMEM((2, rows, samples // 2 + LANES), i16),
+            pltpu.VMEM((C, rows, samples // 2 + LANES), i16),
             pltpu.VMEM((T, rows, samples + LANES), i16),
             pltpu.VMEM((T, rows, samples + LANES), i16),
-            pltpu.VMEM((T, rows, samples + LANES), i16),
+            pltpu.VMEM((2 * T, VS, LANES), f32),
+            pltpu.VMEM((2 * T, rows, samples // 2), i16),
             pltpu.VMEM((rows, T * samples + LAGS + LANES), f32),
             pltpu.VMEM((LAGS // T // FINE * rows, T * samples + LANES), bf16),
-            dma((C,)), dma((C,)), dma((T,)), dma((T,)), dma((T,)), dma((T,)), dma((T,)), dma((T,)),
+            dma((C,)), dma((C,)), dma((T,)), dma((T,)), dma((T,)), dma((T,)),
+            dma((2 * T,)), dma((2 * T,)), dma((T,)), dma((T,)), dma((T,)), dma((T,)),
         ],
         compiler_params=pltpu.CompilerParams(
             collective_id=0, has_side_effects=True,

time: 18.2 us -> 19.4 us (1.066)
  Pallas kernels: 17.3 us -> 18.4 us
    pallas_call x1, Pallas kernels: 17.3 us -> 18.4 us  [shards(): pl.pallas_call(functools.partial(body, C, T, rows), out_shape=pltpu.VMEM(...]
where the time goes in v4:
time: 19.4 us; the launch traced here: 19.1 us
  Pallas kernels  18.4 us (95%)
  local copies, waits for them, and re-layouts  0.71 us (4%)
    pallas_call x1, Pallas kernels, shards(): pl.pallas_call(functools.partial(body, C, T, rows), out_shape=pltpu.VMEM(...  18.4 us
    unnamed x1, local copies, waits for them, and re-layouts  0.71 us

profile of v4, /device:TPU:0, one launch (start us, length us, event | category | flops | bytes accessed | tf_op | source)
XLA Modules:
  0.0 19.1 jit_solution(6668089728927488040)
XLA Ops:
  0.0 18.4 %shard_map.46 = f32[16,16,256]{2,1,0:T(8,128)S(1)} custom-call(f32[32]{0:T(128)} %taps_hbm.1, s32[1,16]{1,0:T(1,128)} %pair_hbm.1, s32[2]{0:T(128)} %blocks_hbm.1, bf16[16,4096]{1,0:T(8,128)(2,1)} %rec_hbm.1), custom_call_target="tpu_custom_call" | custom-call | flops 600000000 | bytes 1000000 | tf_op jit(solution)/shard_map/pallas_call | solution.py:386
  18.4 0.7 %copy.6 = f32[2,8,16,256]{3,2,1,0:T(8,128)} copy(f32[2,8,16,256]{3,2,1,0:T(8,128)S(1)} %bitcast.1) | data formatting | bytes 524288

commit v5 on v4

--- a/solution.py
+++ b/solution.py
@@ -20,8 +20,9 @@
 
 def body(C, T, rows, taps_hbm, pair_hbm, blocks_hbm, rec_hbm, out_ref,
          taps_ref, pair_ref, blocks_ref, rec_ref, local_s,
-         halves, plane, own, partner, small, body_, wp, wall,
-         plane_s, plane_r, own_s, own_r, partner_s, partner_r, small_s, small_r, body_s, body_r, twin_s, twin_r):
+         full, mate, halves, plane, own, partner, facts_w, facts_s, part_s, wp, wall, src,
+         plane_s, plane_r, own_s, own_r, mate_s, mate_r, partner_s, partner_r, fw_s, fw_r, fs_s, fs_r,
+         body_s, body_r, twin_s, twin_r):
     me = lax.axis_index("chan")
     t = lax.axis_index("tm")
     f32, bf16, i16, i32 = jnp.float32, jnp.bfloat16, jnp.int16, jnp.int32
@@ -67,7 +68,9 @@
         n = lax.broadcasted_iota(i32, (8, LANES), 1)
         tap = 4 * n + 3 - row
         cell = jnp.zeros((8, LANES), f32)
+    with jax.named_scope("load_taps"):
         loads[0].wait()
+    with jax.named_scope("band_tiles"):
         for k in range(TAPS):
             cell = jnp.where(tap == k, taps_ref[k], cell)
         reach = TAPS // 4 + 1
@@ -86,6 +89,7 @@
         hi = band.astype(bf16)
         lo = (band - hi.astype(f32)).astype(bf16)
         band2 = jnp.concatenate([hi, lo], axis=1)
+    with jax.named_scope("load_records"):
         for load in loads[1:]:
             load.wait()
 
@@ -132,7 +136,8 @@
         q, e = encode(filtered)
         note = jnp.where(lane == SPILL, e.astype(i32), jnp.where(lane == SPILL + 1, pick, q[:, samples:])).astype(i16)
         q = q[:, :samples].astype(i16)
-        own[t] = jnp.concatenate([q, note], axis=1)
+        own[t] = q
+        full[...] = jnp.concatenate([q, note], axis=1)
         halves[0] = jnp.concatenate([q[:, :part], note], axis=1)
         halves[1] = jnp.concatenate([q[:, part:], note], axis=1)
         plane[me] = halves[side]
@@ -142,7 +147,8 @@
 
     with jax.named_scope("send_filtered"):
         others = [d for d in range(1, C) if d != half]
-        sends = [remote(own.at[t], partner.at[t], partner_s.at[0], partner_r.at[0], {"chan": at_chan(half)})]
+        mate_copy = remote(full, mate, mate_s, mate_r, {"chan": at_chan(half)})
+        sends = [mate_copy]
         sends += [remote(own.at[t], own.at[t], own_s.at[d], own_r.at[d], {"tm": at_tm(d)}) for d in range(1, T)]
         sends += [remote(halves.at[lax.rem(side + d, 2)], plane.at[me], plane_s.at[d], plane_r.at[d],
                          {"chan": at_chan(d)}) for d in others]
@@ -152,6 +158,7 @@
     with jax.named_scope("clear"):
         wp[:, window:] = jnp.zeros((rows, wp.shape[1] - window), f32)
         wall[:, window:] = jnp.zeros((wall.shape[0], LANES), bf16)
+        src[:, :, samples:] = jnp.zeros((T, rows, LANES), f32)
 
     low = t < T // 2
     edge_dist = jnp.where(low, t, T - 1 - t)
@@ -170,6 +177,58 @@
         s.start()
         relays.append(s)
 
+    def tile_of(spill, head, scale, other, power):
+        x = jnp.where(lane < SPILL, spill, jnp.where(lane < 2 * SPILL, pltpu.roll(head, SPILL, 1), jnp.where(
+            lane == 2 * SPILL, scale, jnp.where(lane == 2 * SPILL + 1, other, power))))
+        return jnp.where(lane[:VS] < LANES // 2, x[:VS], pltpu.roll(x[VS:], LANES // 2, 1))
+
+    def facts(ref, at):
+        x = ref[at]
+        return jnp.concatenate([x, pltpu.roll(x, LANES // 2, 1)], axis=0)
+
+    def power_of(x, skip):
+        sq = jnp.where((lane < SPILL) & skip, 0.0, x[:, :LANES] * x[:, :LANES])
+        for g in range(1, x.shape[1] // LANES):
+            y = x[:, LANES * g:LANES * (g + 1)]
+            sq = sq + y * y
+        return jnp.sum(sq, axis=1, keepdims=True)
+
+    def whitening(ref, each):
+        total = jnp.zeros((rows, LANES), f32)
+        before = None
+        for i in range(T):
+            first = facts(ref, each * i)
+            final = facts(ref, each * i + each - 1)
+            head = pltpu.roll(first, LANES - SPILL, 1)
+            if before is not None:
+                head = head + before
+            before = final
+            total = total + jnp.where(lane < SPILL, head * head, jnp.where(
+                lane == 2 * SPILL + 2, first + final if each > 1 else first, 0.0))
+        return lax.rsqrt(jnp.sum(total, axis=1, keepdims=True) / window + 1e-6)
+
+    def spilled(ref, each, slot):
+        return jnp.where((slot > 0) & (lane < SPILL), facts(ref, each * jnp.maximum(slot, 1) - 1), 0.0)
+
+    def fw_copy(d, at):
+        return remote(facts_w.at[at], facts_w.at[at], fw_s.at[d], fw_r.at[d], {"tm": at_tm(d)})
+
+    with jax.named_scope("wait_mate"):
+        mate_copy.wait_recv()
+
+    with jax.named_scope("own_facts"):
+        partner[t] = mate[:, :samples]
+        theirs = permuted(perm, mate[...])
+        mine_scale = jnp.exp2(e - (FULL + 1))
+        mate_scale = jnp.exp2(theirs[:, samples + SPILL:samples + SPILL + 1] - (FULL + 1))
+        x = plain(full[...]) * mine_scale + theirs * mate_scale
+        facts_w[t] = tile_of(x[:, samples:], x[:, :LANES], mine_scale, mate_scale, power_of(x[:, :samples], True))
+        fw_sends = [fw_copy(d, t) for d in range(1, T)]
+        for s in fw_sends:
+            s.start()
+        body_half = jnp.where(side == 0, plain(mate[:, :part]), plain(mate[:, part:samples]))
+        plane[at_chan(half)] = jnp.concatenate([body_half.astype(i32).astype(i16), mate[:, samples:]], axis=1)
+
     with jax.named_scope("relay_first"):
         relay(0)
 
@@ -177,16 +236,12 @@
         for d in others:
             slot = at_chan(C - d)
             remote(halves.at[0], plane.at[slot], plane_s.at[d], plane_r.at[d], {"chan": at_chan(d)}).wait_recv()
-        remote(own.at[t], partner.at[t], partner_s.at[0], partner_r.at[0], {"chan": at_chan(half)}).wait_recv()
 
     with jax.named_scope("relay_rest"):
         for k in range(1, max(1, T - 2)):
             relay(k)
 
     with jax.named_scope("pick"):
-        mate = partner[t]
-        body_half = jnp.where(side == 0, plain(mate[:, :part]), plain(mate[:, part:samples]))
-        plane[at_chan(half)] = jnp.concatenate([body_half.astype(i32).astype(i16), mate[:, samples:]], axis=1)
         picked = []
         per = rows // VS
 
@@ -207,28 +262,20 @@
             picked.append(scaled(mine) + scaled(theirs))
         x = jnp.concatenate(picked, axis=0)
         q, e = encode(x[:, :part])
-        spill, head = x[:, part:], x[:, :LANES]
-        sq = jnp.where((lane < SPILL) & (side == 0), 0.0, head * head)
-        for g in range(1, part // LANES):
-            y = x[:, LANES * g:LANES * (g + 1)]
-            sq = sq + y * y
-        facts = jnp.where(lane < SPILL, spill, jnp.where(lane < 2 * SPILL, pltpu.roll(head, SPILL, 1), jnp.where(
-            lane == 2 * SPILL, jnp.exp2(e - FULL), jnp.sum(sq, axis=1, keepdims=True))))
-        low_lane = lane[:VS] < LANES // 2
         mine_at = 2 * t + side
-        small[mine_at] = jnp.where(low_lane, facts[:VS], pltpu.roll(facts[VS:], LANES // 2, 1))
-        body_[mine_at] = q.astype(i16)
+        facts_s[mine_at] = tile_of(x[:, part:], x[:, :LANES], jnp.exp2(e - FULL), 0.0, power_of(x[:, :part], side == 0))
+        part_s[mine_at] = q.astype(i16)
         away = [(d, p) for d in range(T) for p in range(2) if d or p]
 
         def small_copy(d, p, at):
             where = {"tm": at_tm(d)} if p == 0 else {"chan": twin, "tm": at_tm(d)}
-            return remote(small.at[at], small.at[at], small_s.at[2 * d + p], small_r.at[2 * d + p], where)
+            return remote(facts_s.at[at], facts_s.at[at], fs_s.at[2 * d + p], fs_r.at[2 * d + p], where)
 
         def twin_copy(d, at):
-            return remote(body_.at[at], body_.at[at], twin_s.at[d], twin_r.at[d], {"chan": twin})
+            return remote(part_s.at[at], part_s.at[at], twin_s.at[d], twin_r.at[d], {"chan": twin})
 
         def body_copy(d, at):
-            return remote(body_.at[at], body_.at[at], body_s.at[d], body_r.at[d], {"tm": at_tm(d)})
+            return remote(part_s.at[at], part_s.at[at], body_s.at[d], body_r.at[d], {"tm": at_tm(d)})
 
         ts_sends = [small_copy(d, p, mine_at) for d, p in away if d]
         ts_sends += [body_copy(d, mine_at) for d in range(1, T)]
@@ -240,114 +287,120 @@
         for k in range(max(1, T - 2), T - 1):
             relay(k)
 
-    def assemble(blocks):
-        out = []
-        for i, x in enumerate(blocks):
-            head = x[:, :LANES]
-            if i:
-                head = head + jnp.where(lane < SPILL, blocks[i - 1][:, samples:], 0.0)
-            out.append(jnp.concatenate([head, x[:, LANES:samples]], axis=1))
-        return out
-
-    def whiten(blocks):
-        acc = jnp.zeros((rows, LANES), f32)
-        for x in blocks:
-            sq = x * x
-            for g in range(groups):
-                acc = acc + sq[:, LANES * g:LANES * (g + 1)]
-        scale = lax.rsqrt(jnp.sum(acc, axis=1, keepdims=True) / window + 1e-6)
-        return [(x * scale).astype(bf16) for x in blocks]
-
-    with jax.named_scope("wait_partner"):
-        for k in range(T - 1):
-            slot, d = near(k)
-            remote(partner.at[slot], partner.at[slot], partner_s.at[d], partner_r.at[d],
-                   {"chan": at_chan(half)}).wait_recv()
-
-    with jax.named_scope("white"):
-        white = whiten(assemble([scaled(plain(own[i])) + scaled(permuted(perm, partner[i])) for i in range(T)]))
-        for i in range(T):
-            wp[:, samples * i:samples * (i + 1)] = white[i].astype(f32)
-
-    with jax.named_scope("wall"):
-        lag0 = t * lag_dev
-        wide = samples + LANES * P_
-        if lag_dev % LANES == 0:
-            base, rest = lag0, 0
-        else:
-            base = lax.div(lag0, LANES) * LANES
-            rest = lax.rem(lag0, LANES)
-        for i in range(T):
-            wrows = wp[:, pl.ds(pl.multiple_of(i * samples + base, LANES), wide)]
-            for a in range(A_):
-                rolled = wrows
-                if lag_dev % LANES:
-                    rolled = pltpu.roll(wrows, wide - FINE * a - rest, 1)
-                elif a:
-                    rolled = pltpu.roll(wrows, wide - FINE * a, 1)
-                for p in range(P_):
-                    r0 = (p * A_ + a) * rows
-                    wall[r0:r0 + rows, samples * i:samples * (i + 1)] = (
-                        rolled[:, LANES * p:LANES * p + samples].astype(bf16))
-
-    with jax.named_scope("wait_small"):
+    lag0 = t * lag_dev
+    wide = samples + LANES * P_
+    span = samples + LANES
+    if lag_dev % LANES == 0:
+        base, rest = lag0, 0
+    else:
+        base = lax.div(lag0, LANES) * LANES
+        rest = lax.rem(lag0, LANES)
+
+    def at_block(slot):
+        return pl.multiple_of(slot * samples, LANES)
+
+    def white(slot):
+        tile = facts(facts_w, slot)
+        x = (plain(own[slot]) * tile[:, 2 * SPILL:2 * SPILL + 1]
+             + permuted(perm, partner[slot]) * tile[:, 2 * SPILL + 1:2 * SPILL + 2])
+        x = jnp.concatenate([x[:, :LANES] + spilled(facts_w, 1, slot), x[:, LANES:]], axis=1)
+        wp[:, pl.ds(at_block(slot), samples)] = (x * scale_w).astype(bf16).astype(f32)
+
+    def turn(slot):
+        wrows = wp[:, pl.ds(pl.multiple_of(slot * samples + base, LANES), wide)]
+        for a in range(A_):
+            rolled = wrows
+            if lag_dev % LANES:
+                rolled = pltpu.roll(wrows, wide - FINE * a - rest, 1)
+            elif a:
+                rolled = pltpu.roll(wrows, wide - FINE * a, 1)
+            for p in range(P_):
+                r0 = (p * A_ + a) * rows
+                wall[r0:r0 + rows, pl.ds(at_block(slot), samples)] = (
+                    rolled[:, LANES * p:LANES * p + samples].astype(bf16))
+
+    def source(slot):
+        first, second = facts(facts_s, 2 * slot), facts(facts_s, 2 * slot + 1)
+        x = jnp.concatenate([plain(part_s[2 * slot]) * first[:, 2 * SPILL:2 * SPILL + 1],
+                             plain(part_s[2 * slot + 1]) * second[:, 2 * SPILL:2 * SPILL + 1]], axis=1)
+        x = jnp.concatenate([x[:, :LANES] + spilled(facts_s, 2, slot), x[:, LANES:]], axis=1)
+        src[slot, :, :samples] = (x * scale_s).astype(bf16).astype(f32)
+
+    def term(slot):
+        xs = []
+        for s in range(STEPS * VS):
+            one = jnp.broadcast_to(src[slot, s:s + 1, :], (FINE, span))
+            xs.append(pltpu.roll(one, 0, 1, stride=1, stride_axis=0).astype(bf16))
+        ws = wall[:, pl.ds(at_block(slot), span)]
+        return lax.dot_general(ws, jnp.concatenate(xs, axis=0),
+                               (((1,), (1,)), ((), ())), preferred_element_type=f32)
+
+    def wait_partner(k):
+        slot, d = near(k)
+        remote(partner.at[slot], partner.at[slot], partner_s.at[d], partner_r.at[d],
+               {"chan": at_chan(half)}).wait_recv()
+
+    def hand_to_twin(k):
+        slot, d = near(k)
+        body_copy(d, 2 * slot + side).wait_recv()
+        s = twin_copy(d, 2 * slot + side)
+        s.start()
+        relays.append(s)
+
+    def wait_twin(k):
+        slot, d = near(k)
+        twin_copy(d, 2 * slot + 1 - side).wait_recv()
+
+    with jax.named_scope("wait_own_facts"):
+        for d in range(1, T):
+            fw_copy(d, at_tm(T - d)).wait_recv()
+        scale_w = whitening(facts_w, 1)
+    with jax.named_scope("white_own"):
+        white(t)
+    for k in range(T - 2):
+        with jax.named_scope("wait_partner"):
+            wait_partner(k)
+        with jax.named_scope("white"):
+            white(near(k)[0])
+    start = jnp.where(low, 0, 2)
+    with jax.named_scope("turn"):
+        for i in range(T - 2):
+            turn(start + i)
+    with jax.named_scope("wait_source_facts"):
         for d, p in away:
             from_side = side if p == 0 else 1 - side
             small_copy(d, p, 2 * at_tm(T - d) + from_side).wait_recv()
-
+        scale_s = whitening(facts_s, 2)
     with jax.named_scope("hand_to_twin"):
         for k in range(T - 1):
-            slot, d = near(k)
-            body_copy(d, 2 * slot + side).wait_recv()
-            s = twin_copy(d, 2 * slot + side)
-            s.start()
-            relays.append(s)
-
-    with jax.named_scope("source_power"):
-        def facts_of(at):
-            x = small[at]
-            return jnp.concatenate([x, pltpu.roll(x, LANES // 2, 1)], axis=0)
-
-        total = jnp.zeros((rows, LANES), f32)
-        before = None
-        for i in range(T):
-            first, second = facts_of(2 * i), facts_of(2 * i + 1)
-            head = pltpu.roll(first, LANES - SPILL, 1)
-            if before is not None:
-                head = head + before
-            before = second
-            total = total + jnp.where(lane < SPILL, head * head, jnp.where(lane == 2 * SPILL + 1, first + second, 0.0))
-        source_scale = lax.rsqrt(jnp.sum(total, axis=1, keepdims=True) / window + 1e-6)
-
-    span = samples + LANES
-
-    def term(slot):
-        first, second = facts_of(2 * slot), facts_of(2 * slot + 1)
-        before = jnp.where((slot > 0) & (lane < SPILL), facts_of(2 * jnp.maximum(slot, 1) - 1), 0.0)
-        x = jnp.concatenate([plain(body_[2 * slot]) * first[:, 2 * SPILL:2 * SPILL + 1],
-                             plain(body_[2 * slot + 1]) * second[:, 2 * SPILL:2 * SPILL + 1]], axis=1)
-        x = jnp.concatenate([x[:, :LANES] + before, x[:, LANES:]], axis=1) * source_scale
-        x = x.astype(bf16).astype(f32)
-        srows = jnp.concatenate([x, jnp.zeros((rows, LANES), f32)], axis=1)
-        xs = []
-        for s in range(STEPS * VS):
-            one = jnp.broadcast_to(srows[s:s + 1], (FINE, span))
-            xs.append(pltpu.roll(one, 0, 1, stride=1, stride_axis=0).astype(bf16))
-        ws = wall[:, pl.ds(pl.multiple_of(slot * samples, LANES), span)]
-        return lax.dot_general(ws, jnp.concatenate(xs, axis=0),
-                               (((1,), (1,)), ((), ())), preferred_element_type=f32)
-
-    with jax.named_scope("wait_twin_own"):
+            hand_to_twin(k)
+    with jax.named_scope("wait_partner"):
+        wait_partner(T - 2)
+    with jax.named_scope("white"):
+        white(near(T - 2)[0])
+    with jax.named_scope("turn"):
+        for i in range(2):
+            turn(jnp.where(low, T - 2, 0) + i)
+    with jax.named_scope("wait_twin"):
         twin_copy(0, 2 * t + 1 - side).wait_recv()
+        for k in range(T - 2):
+            wait_twin(k)
+    with jax.named_scope("source"):
+        source(t)
+        for k in range(T - 2):
+            source(near(k)[0])
     with jax.named_scope("correlate"):
-        z = term(t)
-    for k in range(T - 1):
-        slot, d = near(k)
-        with jax.named_scope("wait_twin"):
-            twin_copy(d, 2 * slot + 1 - side).wait_recv()
-        with jax.named_scope("correlate"):
-            z = z + term(slot)
-    z = z * (1.0 / math.sqrt(window))
+        z = term(start)
+        for i in range(1, T - 2):
+            z = z + term(start + i)
+    with jax.named_scope("wait_twin"):
+        wait_twin(T - 2)
+    with jax.named_scope("source"):
+        source(near(T - 2)[0])
+    with jax.named_scope("correlate"):
+        for i in range(2):
+            z = z + term(jnp.where(low, T - 2, 0) + i)
+        z = z * (1.0 / math.sqrt(window))
 
     with jax.named_scope("result"):
         lane_group = lane // FINE
@@ -369,7 +422,7 @@
                     out_ref[lo_s + s, :, LANES * p:LANES * p + span_out] = o[:, :span_out]
 
     with jax.named_scope("wait_sends"):
-        for s in sends + relays + ts_sends:
+        for s in sends + fw_sends + relays + ts_sends:
             s.wait_send()
 
 
@@ -394,15 +447,19 @@
             pltpu.SMEM(source_blocks.shape, jnp.int32),
             pltpu.VMEM(records.shape, bf16),
             dma((4,)),
+            pltpu.VMEM((rows, samples + LANES), i16),
+            pltpu.VMEM((rows, samples + LANES), i16),
             pltpu.VMEM((2, rows, samples // 2 + LANES), i16),
             pltpu.VMEM((C, rows, samples // 2 + LANES), i16),
-            pltpu.VMEM((T, rows, samples + LANES), i16),
-            pltpu.VMEM((T, rows, samples + LANES), i16),
+            pltpu.VMEM((T, rows, samples), i16),
+            pltpu.VMEM((T, rows, samples), i16),
+            pltpu.VMEM((T, VS, LANES), f32),
             pltpu.VMEM((2 * T, VS, LANES), f32),
             pltpu.VMEM((2 * T, rows, samples // 2), i16),
             pltpu.VMEM((rows, T * samples + LAGS + LANES), f32),
             pltpu.VMEM((LAGS // T // FINE * rows, T * samples + LANES), bf16),
-            dma((C,)), dma((C,)), dma((T,)), dma((T,)), dma((T,)), dma((T,)),
+            pltpu.VMEM((T, rows, samples + LANES), f32),
+            dma((C,)), dma((C,)), dma((T,)), dma((T,)), dma, dma, dma((T,)), dma((T,)), dma((T,)), dma((T,)),
             dma((2 * T,)), dma((2 * T,)), dma((T,)), dma((T,)), dma((T,)), dma((T,)),
         ],
         compiler_params=pltpu.CompilerParams(

time: 19.4 us -> 18.9 us (0.974)
  the two profiles are of different devices: /device:TPU:0 before, /device:TPU:1 now
where the time goes in v5:
time: 18.9 us; the launch traced here: 18.7 us
  Pallas kernels  18 us (95%)
  local copies, waits for them, and re-layouts  0.71 us (4%)
    pallas_call x1, Pallas kernels, shards(): pl.pallas_call(functools.partial(body, C, T, rows), out_shape=pltpu.VMEM(...  18 us
    unnamed x1, local copies, waits for them, and re-layouts  0.71 us

profile of v5, /device:TPU:1, one launch (start us, length us, event | category | flops | bytes accessed | tf_op | source)
XLA Modules:
  0.0 18.7 jit_solution(4870009203554211235)
XLA Ops:
  0.0 18.0 %shard_map.46 = f32[16,16,256]{2,1,0:T(8,128)S(1)} custom-call(f32[32]{0:T(128)} %taps_hbm.1, s32[1,16]{1,0:T(1,128)} %pair_hbm.1, s32[2]{0:T(128)} %blocks_hbm.1, bf16[16,4096]{1,0:T(8,128)(2,1)} %rec_hbm.1), custom_call_target="tpu_custom_call" | custom-call | flops 600000000 | bytes 1000000 | tf_op jit(solution)/shard_map/pallas_call | solution.py:439
  18.0 0.7 %copy.6 = f32[2,8,16,256]{3,2,1,0:T(8,128)} copy(f32[2,8,16,256]{3,2,1,0:T(8,128)S(1)} %bitcast.1) | data formatting | bytes 524288

commit v6 on v3

--- a/solution.py
+++ b/solution.py
@@ -20,13 +20,18 @@
 
 def body(C, T, rows, taps_hbm, pair_hbm, blocks_hbm, rec_hbm, out_ref,
          taps_ref, pair_ref, blocks_ref, rec_ref, local_s,
-         plane, own, partner, ts, wp, wall,
-         plane_s, plane_r, own_s, own_r, partner_s, partner_r, ts_s, ts_r):
+         halves, plane, own, partner, part_s, wp, wall,
+         plane_s, plane_r, own_s, own_r, partner_s, partner_r,
+         body_s, body_r, twin_s, twin_r):
     me = lax.axis_index("chan")
     t = lax.axis_index("tm")
     f32, bf16, i16, i32 = jnp.float32, jnp.bfloat16, jnp.int16, jnp.int32
     samples = rec_ref.shape[1] // 4
     width = samples + LANES
+    part = samples // 2
+    half = C // 2
+    side = lax.rem(me, 2)
+    twin = me + 1 - 2 * side
     lag_dev = LAGS // T
     P_ = max(1, lag_dev // LANES)
     A_ = min(lag_dev, LANES) // FINE
@@ -61,7 +66,9 @@
         n = lax.broadcasted_iota(i32, (8, LANES), 1)
         tap = 4 * n + 3 - row
         cell = jnp.zeros((8, LANES), f32)
+    with jax.named_scope("load_taps"):
         loads[0].wait()
+    with jax.named_scope("band_tiles"):
         for k in range(TAPS):
             cell = jnp.where(tap == k, taps_ref[k], cell)
         reach = TAPS // 4 + 1
@@ -80,21 +87,21 @@
         hi = band.astype(bf16)
         lo = (band - hi.astype(f32)).astype(bf16)
         band2 = jnp.concatenate([hi, lo], axis=1)
+    with jax.named_scope("load_records"):
         for load in loads[1:]:
             load.wait()
 
     groups = samples // LANES
     lane = lax.broadcasted_iota(i32, (rows, LANES), 1)
 
-    def encode(x, note):
+    def encode(x):
         peak = jnp.maximum(jnp.max(jnp.abs(x), axis=1, keepdims=True), 1e-30)
         e = jnp.floor(jnp.log2(peak)) + 1.0
-        q = jnp.clip(jnp.round(x * jnp.exp2(FULL - e)), -32767.0, 32767.0).astype(i32)
-        last = jnp.where(lane == SPILL, e.astype(i32), jnp.where(lane == SPILL + 1, note, q[:, samples:]))
-        return jnp.concatenate([q[:, :samples], last], axis=1).astype(i16)
+        return jnp.clip(jnp.round(x * jnp.exp2(FULL - e)), -32767.0, 32767.0).astype(i32), e
 
     def scaled(v):
-        return v * jnp.exp2(v[:, samples + SPILL:samples + SPILL + 1] - (FULL + 1))
+        at = v.shape[1] - LANES + SPILL
+        return v * jnp.exp2(v[:, at:at + 1] - (FULL + 1))
 
     def plain(x):
         return x.astype(i32).astype(f32)
@@ -103,7 +110,7 @@
         v = x.astype(i32)
         pair = jnp.concatenate([(v >> 8).astype(f32).astype(bf16), (v & 255).astype(f32).astype(bf16)], axis=1)
         both = jnp.dot(onehot, pair, preferred_element_type=f32)
-        return 256.0 * both[:, :width] + both[:, width:]
+        return 256.0 * both[:, :x.shape[1]] + both[:, x.shape[1]:]
 
     with jax.named_scope("filter"):
         raw = rec_ref[...]
@@ -124,19 +131,25 @@
         for r in range(rows):
             pick = jnp.where(rr == r, pair_ref[0, r], pick)
         perm = jnp.where(pick[:, :rows] == lax.broadcasted_iota(i32, (rows, rows), 1), 1.0, 0.0).astype(bf16)
-        code = encode(filtered, pick)
-        plane[me] = code
-        own[t] = code
+        q, e = encode(filtered)
+        note = jnp.where(lane == SPILL, e.astype(i32), jnp.where(lane == SPILL + 1, pick, q[:, samples:])).astype(i16)
+        q = q[:, :samples].astype(i16)
+        own[t] = jnp.concatenate([q, note], axis=1)
+        halves[0] = jnp.concatenate([q[:, :part], note], axis=1)
+        halves[1] = jnp.concatenate([q[:, part:], note], axis=1)
+        plane[me] = halves[side]
 
     with jax.named_scope("wait_greeting"):
         pl.semaphore_wait(barrier, C + T - 2)
 
-    half = C // 2
     with jax.named_scope("send_filtered"):
-        order = [half] + [d for d in range(1, C) if d != half]
-        sends = [remote(plane.at[me], plane.at[me], plane_s.at[d], plane_r.at[d], {"chan": at_chan(d)}) for d in order]
+        others = [d for d in range(1, C) if d != half]
+        mate_copy = remote(own.at[t], partner.at[t], partner_s.at[0], partner_r.at[0], {"chan": at_chan(half)})
+        sends = [mate_copy]
+        sends += [remote(halves.at[lax.rem(side + d, 2)], plane.at[me], plane_s.at[d], plane_r.at[d],
+                         {"chan": at_chan(d)}) for d in others]
         sends += [remote(own.at[t], own.at[t], own_s.at[d], own_r.at[d], {"tm": at_tm(d)}) for d in range(1, T)]
-        for s in sends[:1] + sends[C - 1:] + sends[1:C - 1]:
+        for s in sends:
             s.start()
 
     with jax.named_scope("clear"):
@@ -144,11 +157,9 @@
         wall[:, window:] = jnp.zeros((wall.shape[0], LANES), bf16)
 
     low = t < T // 2
-    edge_dist = jnp.where(low, t, T - 1 - t)
-
     def near(k):
-        up = jnp.where(k >= edge_dist, k + 1, k)
-        slot = jnp.where(low, up, T - 1 - up)
+        up = jnp.where(k >= t, k + 1, k)
+        slot = jnp.where(low, up, lax.rem(t - 1 - k + T, T))
         return slot, lax.rem(t - slot + T, T)
 
     relays = []
@@ -160,13 +171,24 @@
         s.start()
         relays.append(s)
 
+    with jax.named_scope("wait_mate"):
+        mate_copy.wait_recv()
+
+    def combine(slot):
+        return scaled(plain(own[slot])) + scaled(permuted(perm, partner[slot]))
+
+    with jax.named_scope("own_block"):
+        mate = partner[t]
+        body_half = jnp.where(side == 0, plain(mate[:, :part]), plain(mate[:, part:samples]))
+        plane[at_chan(half)] = jnp.concatenate([body_half.astype(i32).astype(i16), mate[:, samples:]], axis=1)
+
     with jax.named_scope("relay_first"):
         relay(0)
 
     with jax.named_scope("wait_plane"):
-        for d in order:
+        for d in others:
             slot = at_chan(C - d)
-            remote(plane.at[slot], plane.at[slot], plane_s.at[d], plane_r.at[d], {"chan": at_chan(d)}).wait_recv()
+            remote(halves.at[0], plane.at[slot], plane_s.at[d], plane_r.at[d], {"chan": at_chan(d)}).wait_recv()
 
     with jax.named_scope("pick"):
         picked = []
@@ -183,18 +205,54 @@
             owner = lax.div(blk, per)
             within = lax.rem(blk, per)
             mine = halved(plain(plane[owner]), within)
-            pair = mine[:, samples + SPILL + 1:samples + SPILL + 2]
+            pair = mine[:, part + SPILL + 1:part + SPILL + 2]
             onehot = jnp.where(pair == lax.broadcasted_iota(i32, (VS, rows), 1).astype(f32), 1.0, 0.0).astype(bf16)
             theirs = permuted(onehot, plane[lax.rem(owner + half, C)])
             picked.append(scaled(mine) + scaled(theirs))
-        ts[t] = encode(jnp.concatenate(picked, axis=0), jnp.zeros((rows, LANES), i32))
-        ts_sends = [remote(ts.at[t], ts.at[t], ts_s.at[d], ts_r.at[d], {"tm": at_tm(d)}) for d in range(1, T)]
+        x = jnp.concatenate(picked, axis=0)
+        q, e = encode(x)
+        last = jnp.where(lane == SPILL, e.astype(i32), q[:, part:])
+        mine_at = 2 * t + side
+        part_s[mine_at] = jnp.concatenate([q[:, :part], last], axis=1).astype(i16)
+
+        def twin_copy(d, at):
+            return remote(part_s.at[at], part_s.at[at], twin_s.at[d], twin_r.at[d], {"chan": twin})
+
+        def body_copy(d, at):
+            return remote(part_s.at[at], part_s.at[at], body_s.at[d], body_r.at[d], {"tm": at_tm(d)})
+
+        ts_sends = [body_copy(d, mine_at) for d in range(1, T)] + [twin_copy(0, mine_at)]
         for s in ts_sends:
             s.start()
 
-    with jax.named_scope("relay_rest"):
+    with jax.named_scope("relay"):
         for k in range(1, T - 1):
             relay(k)
+
+    lag0 = t * lag_dev
+    wide = samples + LANES * P_
+    span = samples + LANES
+    if lag_dev % LANES == 0:
+        base, rest = lag0, 0
+    else:
+        base = lax.div(lag0, LANES) * LANES
+        rest = lax.rem(lag0, LANES)
+
+    def wait_partner(k):
+        slot, d = near(k)
+        remote(partner.at[slot], partner.at[slot], partner_s.at[d], partner_r.at[d],
+               {"chan": at_chan(half)}).wait_recv()
+
+    def hand_to_twin(k):
+        slot, d = near(k)
+        body_copy(d, 2 * slot + side).wait_recv()
+        s = twin_copy(d, 2 * slot + side)
+        s.start()
+        relays.append(s)
+
+    def wait_twin(k):
+        slot, d = near(k)
+        twin_copy(d, 2 * slot + 1 - side).wait_recv()
 
     def assemble(blocks):
         out = []
@@ -212,28 +270,19 @@
             for g in range(groups):
                 acc = acc + sq[:, LANES * g:LANES * (g + 1)]
         scale = lax.rsqrt(jnp.sum(acc, axis=1, keepdims=True) / window + 1e-6)
-        return [(x * scale).astype(bf16) for x in blocks]
-
+        return [(x * scale).astype(bf16).astype(f32) for x in blocks]
+
+    with jax.named_scope("hand_to_twin"):
+        for k in range(T - 1):
+            hand_to_twin(k)
     with jax.named_scope("wait_partner"):
-        partner[t] = plane[at_chan(half)]
         for k in range(T - 1):
-            slot, d = near(k)
-            remote(partner.at[slot], partner.at[slot], partner_s.at[d], partner_r.at[d],
-                   {"chan": at_chan(half)}).wait_recv()
-
+            wait_partner(k)
     with jax.named_scope("white"):
-        white = whiten(assemble([scaled(plain(own[i])) + scaled(permuted(perm, partner[i])) for i in range(T)]))
+        white = whiten(assemble([combine(i) for i in range(T)]))
         for i in range(T):
-            wp[:, samples * i:samples * (i + 1)] = white[i].astype(f32)
-
-    with jax.named_scope("wall"):
-        lag0 = t * lag_dev
-        wide = samples + LANES * P_
-        if lag_dev % LANES == 0:
-            base, rest = lag0, 0
-        else:
-            base = lax.div(lag0, LANES) * LANES
-            rest = lax.rem(lag0, LANES)
+            wp[:, samples * i:samples * (i + 1)] = white[i]
+    with jax.named_scope("turn"):
         for i in range(T):
             wrows = wp[:, pl.ds(pl.multiple_of(i * samples + base, LANES), wide)]
             for a in range(A_):
@@ -246,26 +295,25 @@
                     r0 = (p * A_ + a) * rows
                     wall[r0:r0 + rows, samples * i:samples * (i + 1)] = (
                         rolled[:, LANES * p:LANES * p + samples].astype(bf16))
-
-    with jax.named_scope("wait_sources"):
+    with jax.named_scope("wait_twin"):
+        twin_copy(0, 2 * t + 1 - side).wait_recv()
         for k in range(T - 1):
-            slot, d = near(k)
-            remote(ts.at[slot], ts.at[slot], ts_s.at[d], ts_r.at[d], {"tm": at_tm(d)}).wait_recv()
-
+            wait_twin(k)
     with jax.named_scope("sources"):
-        sources = whiten(assemble([2.0 * scaled(plain(ts[i])) for i in range(T)]))
-
-    span = samples + LANES
+        blocks = []
+        for i in range(T):
+            first, second = 2.0 * scaled(plain(part_s[2 * i])), 2.0 * scaled(plain(part_s[2 * i + 1]))
+            blocks.append(jnp.concatenate([first[:, :part], second], axis=1))
+        sources = whiten(assemble(blocks))
     with jax.named_scope("correlate"):
         z = None
         for i in range(T):
-            srows = jnp.concatenate([sources[i].astype(f32), jnp.zeros((rows, LANES), f32)], axis=1)
+            srows = jnp.concatenate([sources[i], jnp.zeros((rows, LANES), f32)], axis=1)
             xs = []
             for s in range(STEPS * VS):
                 one = jnp.broadcast_to(srows[s:s + 1], (FINE, span))
                 xs.append(pltpu.roll(one, 0, 1, stride=1, stride_axis=0).astype(bf16))
-            ws = wall[:, samples * i:samples * i + span]
-            term = lax.dot_general(ws, jnp.concatenate(xs, axis=0),
+            term = lax.dot_general(wall[:, samples * i:samples * i + span], jnp.concatenate(xs, axis=0),
                                    (((1,), (1,)), ((), ())), preferred_element_type=f32)
             z = term if z is None else z + term
         z = z * (1.0 / math.sqrt(window))
@@ -315,13 +363,14 @@
             pltpu.SMEM(source_blocks.shape, jnp.int32),
             pltpu.VMEM(records.shape, bf16),
             dma((4,)),
-            pltpu.VMEM((C, rows, samples + LANES), i16),
+            pltpu.VMEM((2, rows, samples // 2 + LANES), i16),
+            pltpu.VMEM((C, rows, samples // 2 + LANES), i16),
             pltpu.VMEM((T, rows, samples + LANES), i16),
             pltpu.VMEM((T, rows, samples + LANES), i16),
-            pltpu.VMEM((T, rows, samples + LANES), i16),
+            pltpu.VMEM((2 * T, rows, samples // 2 + LANES), i16),
             pltpu.VMEM((rows, T * samples + LAGS + LANES), f32),
             pltpu.VMEM((LAGS // T // FINE * rows, T * samples + LANES), bf16),
-            dma((C,)), dma((C,)), dma((T,)), dma((T,)), dma((T,)), dma((T,)), dma((T,)), dma((T,)),
+            dma((C,)), dma((C,)), dma((T,)), dma((T,)), dma((T,)), dma((T,)), dma((T,)), dma((T,)), dma((T,)), dma((T,)),
         ],
         compiler_params=pltpu.CompilerParams(
             collective_id=0, has_side_effects=True,

time: 18.2 us -> 17.2 us (0.945)
  Pallas kernels: 17.3 us -> 16.3 us
    pallas_call x1, Pallas kernels: 17.3 us -> 16.3 us  [shards(): pl.pallas_call(functools.partial(body, C, T, rows), out_shape=pltpu.VMEM(...]
where the time goes in v6:
time: 17.2 us; the launch traced here: 17 us
  Pallas kernels  16.3 us (95%)
  local copies, waits for them, and re-layouts  0.71 us (4%)
    pallas_call x1, Pallas kernels, shards(): pl.pallas_call(functools.partial(body, C, T, rows), out_shape=pltpu.VMEM(...  16.3 us
    unnamed x1, local copies, waits for them, and re-layouts  0.71 us

profile of v6, /device:TPU:0, one launch (start us, length us, event | category | flops | bytes accessed | tf_op | source)
XLA Modules:
  0.0 17.0 jit_solution(10486894880867282196)
XLA Ops:
  0.0 16.3 %shard_map.46 = f32[16,16,256]{2,1,0:T(8,128)S(1)} custom-call(f32[32]{0:T(128)} %taps_hbm.1, s32[1,16]{1,0:T(1,128)} %pair_hbm.1, s32[2]{0:T(128)} %blocks_hbm.1, bf16[16,4096]{1,0:T(8,128)(2,1)} %rec_hbm.1), custom_call_target="tpu_custom_call" | custom-call | flops 600000000 | bytes 1000000 | tf_op jit(solution)/shard_map/pallas_call | solution.py:355
  16.3 0.7 %copy.6 = f32[2,8,16,256]{3,2,1,0:T(8,128)} copy(f32[2,8,16,256]{3,2,1,0:T(8,128)S(1)} %bitcast.1) | data formatting | bytes 524288

commit v7 on v6

--- a/solution.py
+++ b/solution.py
@@ -20,8 +20,8 @@
 
 def body(C, T, rows, taps_hbm, pair_hbm, blocks_hbm, rec_hbm, out_ref,
          taps_ref, pair_ref, blocks_ref, rec_ref, local_s,
-         halves, plane, own, partner, part_s, wp, wall,
-         plane_s, plane_r, own_s, own_r, partner_s, partner_r,
+         halves, plane, mate_rest, own, partner, part_s, wp, wall,
+         plane_s, plane_r, own_s, own_r, mate_s, mate_r, partner_s, partner_r,
          body_s, body_r, twin_s, twin_r):
     me = lax.axis_index("chan")
     t = lax.axis_index("tm")
@@ -47,6 +47,12 @@
         return pltpu.make_async_remote_copy(
             src_ref=src, dst_ref=dst, send_sem=ssem, recv_sem=rsem,
             device_id=where, device_id_type=pl.DeviceIdType.MESH)
+
+    def arrived(buf, count, sem):
+        blocks = buf.at[pl.ds(0, count)]
+        pltpu.make_async_copy(blocks, blocks, sem).wait()
+
+    gone = arrived
 
     with jax.named_scope("greet"):
         loads = [pltpu.make_async_copy(src, dst, local_s.at[i]) for i, (src, dst) in enumerate((
@@ -106,11 +112,20 @@
     def plain(x):
         return x.astype(i32).astype(f32)
 
-    def permuted(onehot, x):
-        v = x.astype(i32)
-        pair = jnp.concatenate([(v >> 8).astype(f32).astype(bf16), (v & 255).astype(f32).astype(bf16)], axis=1)
-        both = jnp.dot(onehot, pair, preferred_element_type=f32)
-        return 256.0 * both[:, :x.shape[1]] + both[:, x.shape[1]:]
+    def permuted(at, x):
+        out = []
+        for h in range(at.shape[0] // 8):
+            want = at[8 * h:8 * h + 8]
+            cols = []
+            for g in range(x.shape[1] // LANES):
+                tile = x[:, LANES * g:LANES * (g + 1)]
+                got = jnp.take_along_axis(tile[:8], want & 7, axis=0)
+                for v in range(1, rows // 8):
+                    more = jnp.take_along_axis(tile[8 * v:8 * v + 8], want & 7, axis=0)
+                    got = jnp.where((want >> 3) == v, more, got)
+                cols.append(got)
+            out.append(jnp.concatenate(cols, axis=1))
+        return jnp.concatenate(out, axis=0)
 
     with jax.named_scope("filter"):
         raw = rec_ref[...]
@@ -130,7 +145,6 @@
         pick = jnp.zeros((rows, LANES), i32)
         for r in range(rows):
             pick = jnp.where(rr == r, pair_ref[0, r], pick)
-        perm = jnp.where(pick[:, :rows] == lax.broadcasted_iota(i32, (rows, rows), 1), 1.0, 0.0).astype(bf16)
         q, e = encode(filtered)
         note = jnp.where(lane == SPILL, e.astype(i32), jnp.where(lane == SPILL + 1, pick, q[:, samples:])).astype(i16)
         q = q[:, :samples].astype(i16)
@@ -144,11 +158,12 @@
 
     with jax.named_scope("send_filtered"):
         others = [d for d in range(1, C) if d != half]
-        mate_copy = remote(own.at[t], partner.at[t], partner_s.at[0], partner_r.at[0], {"chan": at_chan(half)})
-        sends = [mate_copy]
-        sends += [remote(halves.at[lax.rem(side + d, 2)], plane.at[me], plane_s.at[d], plane_r.at[d],
+        mate_copy = remote(halves.at[lax.rem(side + half + 1, 2)], mate_rest, mate_s, mate_r, {"chan": at_chan(half)})
+        others = [half] + others
+        sends = [remote(halves.at[lax.rem(side + d, 2)], plane.at[me], plane_s, plane_r,
                          {"chan": at_chan(d)}) for d in others]
-        sends += [remote(own.at[t], own.at[t], own_s.at[d], own_r.at[d], {"tm": at_tm(d)}) for d in range(1, T)]
+        sends += [remote(own.at[t], own.at[t], own_s, own_r.at[d], {"tm": at_tm(d)}) for d in range(1, T)]
+        sends = sends[:C - 1] + [mate_copy] + sends[C - 1:]
         for s in sends:
             s.start()
 
@@ -162,33 +177,27 @@
         slot = jnp.where(low, up, lax.rem(t - 1 - k + T, T))
         return slot, lax.rem(t - slot + T, T)
 
-    relays = []
-
     def relay(k):
         slot, d = near(k)
-        remote(own.at[slot], own.at[slot], own_s.at[d], own_r.at[d], {"tm": at_tm(d)}).wait_recv()
-        s = remote(own.at[slot], partner.at[slot], partner_s.at[d], partner_r.at[d], {"chan": at_chan(half)})
+        remote(own.at[slot], own.at[slot], own_s, own_r.at[d], {"tm": at_tm(d)}).wait_recv()
+        s = remote(own.at[slot], partner.at[slot], partner_s, partner_r, {"chan": at_chan(half)})
         s.start()
-        relays.append(s)
-
-    with jax.named_scope("wait_mate"):
-        mate_copy.wait_recv()
 
     def combine(slot):
-        return scaled(plain(own[slot])) + scaled(permuted(perm, partner[slot]))
-
-    with jax.named_scope("own_block"):
-        mate = partner[t]
-        body_half = jnp.where(side == 0, plain(mate[:, :part]), plain(mate[:, part:samples]))
-        plane[at_chan(half)] = jnp.concatenate([body_half.astype(i32).astype(i16), mate[:, samples:]], axis=1)
+        return scaled(plain(own[slot])) + scaled(permuted(pick, plain(partner[slot])))
 
     with jax.named_scope("relay_first"):
         relay(0)
 
     with jax.named_scope("wait_plane"):
-        for d in others:
-            slot = at_chan(C - d)
-            remote(halves.at[0], plane.at[slot], plane_s.at[d], plane_r.at[d], {"chan": at_chan(d)}).wait_recv()
+        arrived(plane, C - 1, plane_r)
+
+    early = range(1, min(2, T - 1))
+    with jax.named_scope("relay_early"):
+        @pl.when(low)
+        def _():
+            for k in early:
+                relay(k)
 
     with jax.named_scope("pick"):
         picked = []
@@ -205,28 +214,33 @@
             owner = lax.div(blk, per)
             within = lax.rem(blk, per)
             mine = halved(plain(plane[owner]), within)
-            pair = mine[:, part + SPILL + 1:part + SPILL + 2]
-            onehot = jnp.where(pair == lax.broadcasted_iota(i32, (VS, rows), 1).astype(f32), 1.0, 0.0).astype(bf16)
-            theirs = permuted(onehot, plane[lax.rem(owner + half, C)])
-            picked.append(scaled(mine) + scaled(theirs))
-        x = jnp.concatenate(picked, axis=0)
-        q, e = encode(x)
-        last = jnp.where(lane == SPILL, e.astype(i32), q[:, part:])
+            pair = mine[:, part + SPILL + 1:part + SPILL + 2].astype(i32)
+            theirs = permuted(jnp.broadcast_to(pair, (VS, LANES)), plain(plane[lax.rem(owner + half, C)]))
+            first, second = (x[:, part + SPILL:part + SPILL + 1] for x in (mine, theirs))
+            top = jnp.maximum(first, second)
+            q = jnp.round(mine * jnp.exp2(first - top - 1.0) + theirs * jnp.exp2(second - top - 1.0))
+            last = jnp.where(lane[:VS] == SPILL, top, q[:, part:])
+            picked.append(jnp.concatenate([q[:, :part], last], axis=1))
+        x = jnp.concatenate(picked, axis=0).astype(i32).astype(i16)
         mine_at = 2 * t + side
-        part_s[mine_at] = jnp.concatenate([q[:, :part], last], axis=1).astype(i16)
+        part_s[mine_at] = x
 
         def twin_copy(d, at):
-            return remote(part_s.at[at], part_s.at[at], twin_s.at[d], twin_r.at[d], {"chan": twin})
+            return remote(part_s.at[at], part_s.at[at], twin_s, twin_r, {"chan": twin})
 
         def body_copy(d, at):
-            return remote(part_s.at[at], part_s.at[at], body_s.at[d], body_r.at[d], {"tm": at_tm(d)})
+            return remote(part_s.at[at], part_s.at[at], body_s, body_r.at[d], {"tm": at_tm(d)})
 
         ts_sends = [body_copy(d, mine_at) for d in range(1, T)] + [twin_copy(0, mine_at)]
         for s in ts_sends:
             s.start()
 
     with jax.named_scope("relay"):
-        for k in range(1, T - 1):
+        @pl.when(jnp.logical_not(low))
+        def _():
+            for k in early:
+                relay(k)
+        for k in range(early.stop, T - 1):
             relay(k)
 
     lag0 = t * lag_dev
@@ -238,21 +252,11 @@
         base = lax.div(lag0, LANES) * LANES
         rest = lax.rem(lag0, LANES)
 
-    def wait_partner(k):
-        slot, d = near(k)
-        remote(partner.at[slot], partner.at[slot], partner_s.at[d], partner_r.at[d],
-               {"chan": at_chan(half)}).wait_recv()
-
     def hand_to_twin(k):
         slot, d = near(k)
         body_copy(d, 2 * slot + side).wait_recv()
         s = twin_copy(d, 2 * slot + side)
         s.start()
-        relays.append(s)
-
-    def wait_twin(k):
-        slot, d = near(k)
-        twin_copy(d, 2 * slot + 1 - side).wait_recv()
 
     def assemble(blocks):
         out = []
@@ -275,9 +279,16 @@
     with jax.named_scope("hand_to_twin"):
         for k in range(T - 1):
             hand_to_twin(k)
+    with jax.named_scope("own_block"):
+        mate_copy.wait_recv()
+        near_half, far_half = plain(plane[at_chan(half)]), plain(mate_rest[...])
+        mate = jnp.concatenate([jnp.where(side == 0, near_half[:, :part], far_half[:, :part]),
+                                jnp.where(side == 0, far_half[:, :part], near_half[:, :part]),
+                                near_half[:, part:]], axis=1)
+        partner[t] = mate.astype(i32).astype(i16)
+
     with jax.named_scope("wait_partner"):
-        for k in range(T - 1):
-            wait_partner(k)
+        arrived(partner, T - 1, partner_r)
     with jax.named_scope("white"):
         white = whiten(assemble([combine(i) for i in range(T)]))
         for i in range(T):
@@ -296,9 +307,7 @@
                     wall[r0:r0 + rows, samples * i:samples * (i + 1)] = (
                         rolled[:, LANES * p:LANES * p + samples].astype(bf16))
     with jax.named_scope("wait_twin"):
-        twin_copy(0, 2 * t + 1 - side).wait_recv()
-        for k in range(T - 1):
-            wait_twin(k)
+        arrived(part_s, T, twin_r)
     with jax.named_scope("sources"):
         blocks = []
         for i in range(T):
@@ -338,8 +347,10 @@
                     out_ref[lo_s + s, :, LANES * p:LANES * p + span_out] = o[:, :span_out]
 
     with jax.named_scope("wait_sends"):
-        for s in sends + relays + ts_sends:
-            s.wait_send()
+        mate_copy.wait_send()
+        for buf, count, sem in ((plane, C - 1, plane_s), (own, T - 1, own_s), (partner, T - 1, partner_s),
+                                (part_s, T - 1, body_s), (part_s, T, twin_s)):
+            gone(buf, count, sem)
 
 
 def shards(records, pair_rows, fir_taps, source_blocks):
@@ -365,12 +376,13 @@
             dma((4,)),
             pltpu.VMEM((2, rows, samples // 2 + LANES), i16),
             pltpu.VMEM((C, rows, samples // 2 + LANES), i16),
+            pltpu.VMEM((rows, samples // 2 + LANES), i16),
             pltpu.VMEM((T, rows, samples + LANES), i16),
             pltpu.VMEM((T, rows, samples + LANES), i16),
             pltpu.VMEM((2 * T, rows, samples // 2 + LANES), i16),
             pltpu.VMEM((rows, T * samples + LAGS + LANES), f32),
             pltpu.VMEM((LAGS // T // FINE * rows, T * samples + LANES), bf16),
-            dma((C,)), dma((C,)), dma((T,)), dma((T,)), dma((T,)), dma((T,)), dma((T,)), dma((T,)), dma((T,)), dma((T,)),
+            dma, dma, dma, dma((T,)), dma, dma, dma, dma, dma, dma((T,)), dma, dma,
         ],
         compiler_params=pltpu.CompilerParams(
             collective_id=0, has_side_effects=True,

time: 17.2 us -> 16.6 us (0.965)
  Pallas kernels: 16.3 us -> 15.8 us
    pallas_call x1, Pallas kernels: 16.3 us -> 15.8 us  [shards(): pl.pallas_call(functools.partial(body, C, T, rows), out_shape=pltpu.VMEM(...]
where the time goes in v7:
time: 16.6 us; the launch traced here: 16.5 us
  Pallas kernels  15.8 us (95%)
  local copies, waits for them, and re-layouts  0.71 us (4%)
    pallas_call x1, Pallas kernels, shards(): pl.pallas_call(functools.partial(body, C, T, rows), out_shape=pltpu.VMEM(...  15.8 us
    unnamed x1, local copies, waits for them, and re-layouts  0.71 us

profile of v7, /device:TPU:0, one launch (start us, length us, event | category | flops | bytes accessed | tf_op | source)
XLA Modules:
  0.0 16.5 jit_solution(5920349215442271301)
XLA Ops:
  0.0 15.8 %shard_map.46 = f32[16,16,256]{2,1,0:T(8,128)S(1)} custom-call(f32[32]{0:T(128)} %taps_hbm.1, s32[1,16]{1,0:T(1,128)} %pair_hbm.1, s32[2]{0:T(128)} %blocks_hbm.1, bf16[16,4096]{1,0:T(8,128)(2,1)} %rec_hbm.1), custom_call_target="tpu_custom_call" | custom-call | flops 600000000 | bytes 1000000 | tf_op jit(solution)/shard_map/pallas_call | solution.py:366
  15.8 0.7 %copy.6 = f32[2,8,16,256]{3,2,1,0:T(8,128)} copy(f32[2,8,16,256]{3,2,1,0:T(8,128)S(1)} %bitcast.1) | data formatting | bytes 524288

commit v8 on v7

--- a/solution.py
+++ b/solution.py
@@ -168,8 +168,8 @@
             s.start()
 
     with jax.named_scope("clear"):
-        wp[:, window:] = jnp.zeros((rows, wp.shape[1] - window), f32)
-        wall[:, window:] = jnp.zeros((wall.shape[0], LANES), bf16)
+        wp[:, window:] = jnp.zeros((rows, wp.shape[1] - window), bf16)
+        wall[:, window:] = jnp.zeros((wall.shape[0], LANES * P_), bf16)
 
     low = t < T // 2
     def near(k):
@@ -244,7 +244,7 @@
             relay(k)
 
     lag0 = t * lag_dev
-    wide = samples + LANES * P_
+    wide = samples + LANES
     span = samples + LANES
     if lag_dev % LANES == 0:
         base, rest = lag0, 0
@@ -274,7 +274,7 @@
             for g in range(groups):
                 acc = acc + sq[:, LANES * g:LANES * (g + 1)]
         scale = lax.rsqrt(jnp.sum(acc, axis=1, keepdims=True) / window + 1e-6)
-        return [(x * scale).astype(bf16).astype(f32) for x in blocks]
+        return [(x * scale).astype(bf16) for x in blocks]
 
     with jax.named_scope("hand_to_twin"):
         for k in range(T - 1):
@@ -302,10 +302,7 @@
                     rolled = pltpu.roll(wrows, wide - FINE * a - rest, 1)
                 elif a:
                     rolled = pltpu.roll(wrows, wide - FINE * a, 1)
-                for p in range(P_):
-                    r0 = (p * A_ + a) * rows
-                    wall[r0:r0 + rows, samples * i:samples * (i + 1)] = (
-                        rolled[:, LANES * p:LANES * p + samples].astype(bf16))
+                wall[a * rows:(a + 1) * rows, samples * i:samples * (i + 1)] = rolled[:, :samples]
     with jax.named_scope("wait_twin"):
         arrived(part_s, T, twin_r)
     with jax.named_scope("sources"):
@@ -317,12 +314,14 @@
     with jax.named_scope("correlate"):
         z = None
         for i in range(T):
-            srows = jnp.concatenate([sources[i], jnp.zeros((rows, LANES), f32)], axis=1)
+            srows = jnp.concatenate([sources[i], jnp.zeros((rows, LANES), bf16)], axis=1)
             xs = []
             for s in range(STEPS * VS):
                 one = jnp.broadcast_to(srows[s:s + 1], (FINE, span))
-                xs.append(pltpu.roll(one, 0, 1, stride=1, stride_axis=0).astype(bf16))
-            term = lax.dot_general(wall[:, samples * i:samples * i + span], jnp.concatenate(xs, axis=0),
+                xs.append(pltpu.roll(one, 0, 1, stride=1, stride_axis=0))
+            ws = jnp.concatenate([wall[:, samples * i + LANES * p:samples * i + LANES * p + span] for p in range(P_)],
+                                 axis=0)
+            term = lax.dot_general(ws, jnp.concatenate(xs, axis=0),
                                    (((1,), (1,)), ((), ())), preferred_element_type=f32)
             z = term if z is None else z + term
         z = z * (1.0 / math.sqrt(window))
@@ -380,8 +379,8 @@
             pltpu.VMEM((T, rows, samples + LANES), i16),
             pltpu.VMEM((T, rows, samples + LANES), i16),
             pltpu.VMEM((2 * T, rows, samples // 2 + LANES), i16),
-            pltpu.VMEM((rows, T * samples + LAGS + LANES), f32),
-            pltpu.VMEM((LAGS // T // FINE * rows, T * samples + LANES), bf16),
+            pltpu.VMEM((rows, T * samples + LAGS + LANES), bf16),
+            pltpu.VMEM((min(LAGS // T, LANES) // FINE * rows, T * samples + LANES * max(1, LAGS // T // LANES)), bf16),
             dma, dma, dma, dma((T,)), dma, dma, dma, dma, dma, dma((T,)), dma, dma,
         ],
         compiler_params=pltpu.CompilerParams(

time: 16.6 us -> 16.4 us (0.988)
  Pallas kernels: 15.8 us -> 15.6 us
    pallas_call x1, Pallas kernels: 15.8 us -> 15.6 us  [shards(): pl.pallas_call(functools.partial(body, C, T, rows), out_shape=pltpu.VMEM(...]
where the time goes in v8:
time: 16.4 us; the launch traced here: 16.3 us
  Pallas kernels  15.6 us (95%)
  local copies, waits for them, and re-layouts  0.71 us (4%)
    pallas_call x1, Pallas kernels, shards(): pl.pallas_call(functools.partial(body, C, T, rows), out_shape=pltpu.VMEM(...  15.6 us
    unnamed x1, local copies, waits for them, and re-layouts  0.71 us

profile of v8, /device:TPU:0, one launch (start us, length us, event | category | flops | bytes accessed | tf_op | source)
XLA Modules:
  0.0 16.3 jit_solution(18022039239956856622)
XLA Ops:
  0.0 15.6 %shard_map.46 = f32[16,16,256]{2,1,0:T(8,128)S(1)} custom-call(f32[32]{0:T(128)} %taps_hbm.1, s32[1,16]{1,0:T(1,128)} %pair_hbm.1, s32[2]{0:T(128)} %blocks_hbm.1, bf16[16,4096]{1,0:T(8,128)(2,1)} %rec_hbm.1), custom_call_target="tpu_custom_call" | custom-call | flops 600000000 | bytes 1000000 | tf_op jit(solution)/shard_map/pallas_call | solution.py:365
  15.6 0.7 %copy.6 = f32[2,8,16,256]{3,2,1,0:T(8,128)} copy(f32[2,8,16,256]{3,2,1,0:T(8,128)S(1)} %bitcast.1) | data formatting | bytes 524288

commit v9 on v8

--- a/solution.py
+++ b/solution.py
@@ -20,9 +20,9 @@
 
 def body(C, T, rows, taps_hbm, pair_hbm, blocks_hbm, rec_hbm, out_ref,
          taps_ref, pair_ref, blocks_ref, rec_ref, local_s,
-         halves, plane, mate_rest, own, partner, part_s, wp, wall,
-         plane_s, plane_r, own_s, own_r, mate_s, mate_r, partner_s, partner_r,
-         body_s, body_r, twin_s, twin_r):
+         halves, plane, mate_rest, own, partner, part_s, src, wp, wall,
+         plane_s, plane_r, own_s, own_r, mate_r, partner_s, partner_r,
+         body_r, twin_s, twin_r):
     me = lax.axis_index("chan")
     t = lax.axis_index("tm")
     f32, bf16, i16, i32 = jnp.float32, jnp.bfloat16, jnp.int16, jnp.int32
@@ -57,8 +57,12 @@
     with jax.named_scope("greet"):
         loads = [pltpu.make_async_copy(src, dst, local_s.at[i]) for i, (src, dst) in enumerate((
             (taps_hbm, taps_ref), (rec_hbm, rec_ref), (pair_hbm, pair_ref), (blocks_hbm, blocks_ref)))]
-        for load in loads:
-            load.start()
+        loads[0].start()
+        for g in range(4):
+            cut = pl.ds(samples * g, samples)
+            pltpu.make_async_copy(rec_hbm.at[:, cut], rec_ref.at[:, cut], local_s.at[1]).start()
+        loads[2].start()
+        loads[3].start()
         barrier = pltpu.get_barrier_semaphore()
         for d in range(1, C):
             pl.semaphore_signal(barrier, inc=1, device_id={"chan": at_chan(d)}, device_id_type=pl.DeviceIdType.MESH)
@@ -158,11 +162,11 @@
 
     with jax.named_scope("send_filtered"):
         others = [d for d in range(1, C) if d != half]
-        mate_copy = remote(halves.at[lax.rem(side + half + 1, 2)], mate_rest, mate_s, mate_r, {"chan": at_chan(half)})
+        mate_copy = remote(halves.at[lax.rem(side + half + 1, 2)], mate_rest, plane_s, mate_r, {"chan": at_chan(half)})
         others = [half] + others
         sends = [remote(halves.at[lax.rem(side + d, 2)], plane.at[me], plane_s, plane_r,
                          {"chan": at_chan(d)}) for d in others]
-        sends += [remote(own.at[t], own.at[t], own_s, own_r.at[d], {"tm": at_tm(d)}) for d in range(1, T)]
+        sends += [remote(own.at[t], own.at[t], own_s, own_r.at[d - 1], {"tm": at_tm(d)}) for d in range(1, T)]
         sends = sends[:C - 1] + [mate_copy] + sends[C - 1:]
         for s in sends:
             s.start()
@@ -179,7 +183,7 @@
 
     def relay(k):
         slot, d = near(k)
-        remote(own.at[slot], own.at[slot], own_s, own_r.at[d], {"tm": at_tm(d)}).wait_recv()
+        remote(own.at[slot], own.at[slot], own_s, own_r.at[d - 1], {"tm": at_tm(d)}).wait_recv()
         s = remote(own.at[slot], partner.at[slot], partner_s, partner_r, {"chan": at_chan(half)})
         s.start()
 
@@ -229,7 +233,7 @@
             return remote(part_s.at[at], part_s.at[at], twin_s, twin_r, {"chan": twin})
 
         def body_copy(d, at):
-            return remote(part_s.at[at], part_s.at[at], body_s, body_r.at[d], {"tm": at_tm(d)})
+            return remote(part_s.at[at], part_s.at[at], twin_s, body_r.at[d - 1], {"tm": at_tm(d)})
 
         ts_sends = [body_copy(d, mine_at) for d in range(1, T)] + [twin_copy(0, mine_at)]
         for s in ts_sends:
@@ -255,8 +259,7 @@
     def hand_to_twin(k):
         slot, d = near(k)
         body_copy(d, 2 * slot + side).wait_recv()
-        s = twin_copy(d, 2 * slot + side)
-        s.start()
+        twin_copy(d, 2 * slot + side).start()
 
     def assemble(blocks):
         out = []
@@ -287,13 +290,12 @@
                                 near_half[:, part:]], axis=1)
         partner[t] = mate.astype(i32).astype(i16)
 
-    with jax.named_scope("wait_partner"):
-        arrived(partner, T - 1, partner_r)
-    with jax.named_scope("white"):
+    def whiten_own():
         white = whiten(assemble([combine(i) for i in range(T)]))
         for i in range(T):
             wp[:, samples * i:samples * (i + 1)] = white[i]
-    with jax.named_scope("turn"):
+
+    def turn_own():
         for i in range(T):
             wrows = wp[:, pl.ds(pl.multiple_of(i * samples + base, LANES), wide)]
             for a in range(A_):
@@ -303,23 +305,47 @@
                 elif a:
                     rolled = pltpu.roll(wrows, wide - FINE * a, 1)
                 wall[a * rows:(a + 1) * rows, samples * i:samples * (i + 1)] = rolled[:, :samples]
-    with jax.named_scope("wait_twin"):
-        arrived(part_s, T, twin_r)
-    with jax.named_scope("sources"):
+
+    def whiten_sources():
         blocks = []
         for i in range(T):
             first, second = 2.0 * scaled(plain(part_s[2 * i])), 2.0 * scaled(plain(part_s[2 * i + 1]))
             blocks.append(jnp.concatenate([first[:, :part], second], axis=1))
-        sources = whiten(assemble(blocks))
+        for i, x in enumerate(whiten(assemble(blocks))):
+            src[i] = x
+
+    @pl.when(side == 0)
+    def _():
+        with jax.named_scope("wait_both"):
+            arrived(partner, T - 1, partner_r)
+            arrived(part_s, T, twin_r)
+        with jax.named_scope("prepare_both"):
+            whiten_own()
+            whiten_sources()
+            turn_own()
+
+    @pl.when(side == 1)
+    def _():
+        with jax.named_scope("wait_partner"):
+            arrived(partner, T - 1, partner_r)
+        with jax.named_scope("prepare_own"):
+            whiten_own()
+            turn_own()
+        with jax.named_scope("wait_twin"):
+            arrived(part_s, T, twin_r)
+        with jax.named_scope("prepare_sources"):
+            whiten_sources()
+
     with jax.named_scope("correlate"):
         z = None
         for i in range(T):
-            srows = jnp.concatenate([sources[i], jnp.zeros((rows, LANES), bf16)], axis=1)
+            before = src[i - 1][:, samples - LANES:] if i else jnp.zeros((rows, LANES), bf16)
+            srows = jnp.concatenate([src[i], before], axis=1)
             xs = []
             for s in range(STEPS * VS):
                 one = jnp.broadcast_to(srows[s:s + 1], (FINE, span))
-                xs.append(pltpu.roll(one, 0, 1, stride=1, stride_axis=0))
-            ws = jnp.concatenate([wall[:, samples * i + LANES * p:samples * i + LANES * p + span] for p in range(P_)],
+                xs.append(pltpu.roll(one, 0, 1, stride=1, stride_axis=0)[:, :samples])
+            ws = jnp.concatenate([wall[:, samples * i + LANES * p:samples * i + LANES * p + samples] for p in range(P_)],
                                  axis=0)
             term = lax.dot_general(ws, jnp.concatenate(xs, axis=0),
                                    (((1,), (1,)), ((), ())), preferred_element_type=f32)
@@ -346,9 +372,8 @@
                     out_ref[lo_s + s, :, LANES * p:LANES * p + span_out] = o[:, :span_out]
 
     with jax.named_scope("wait_sends"):
-        mate_copy.wait_send()
-        for buf, count, sem in ((plane, C - 1, plane_s), (own, T - 1, own_s), (partner, T - 1, partner_s),
-                                (part_s, T - 1, body_s), (part_s, T, twin_s)):
+        for buf, count, sem in ((plane, C, plane_s), (own, T - 1, own_s), (partner, T - 1, partner_s),
+                                (part_s, 2 * T - 1, twin_s)):
             gone(buf, count, sem)
 
 
@@ -379,9 +404,10 @@
             pltpu.VMEM((T, rows, samples + LANES), i16),
             pltpu.VMEM((T, rows, samples + LANES), i16),
             pltpu.VMEM((2 * T, rows, samples // 2 + LANES), i16),
+            pltpu.VMEM((T, rows, samples), bf16),
             pltpu.VMEM((rows, T * samples + LAGS + LANES), bf16),
             pltpu.VMEM((min(LAGS // T, LANES) // FINE * rows, T * samples + LANES * max(1, LAGS // T // LANES)), bf16),
-            dma, dma, dma, dma((T,)), dma, dma, dma, dma, dma, dma((T,)), dma, dma,
+            dma, dma, dma, dma((T - 1,)), dma, dma, dma, dma((T - 1,)), dma, dma,
         ],
         compiler_params=pltpu.CompilerParams(
             collective_id=0, has_side_effects=True,

time: 16.4 us -> 16.3 us (level)
  Pallas kernels: 15.6 us -> 15.4 us
    pallas_call x1, Pallas kernels: 15.6 us -> 15.4 us  [shards(): pl.pallas_call(functools.partial(body, C, T, rows), out_shape=pltpu.VMEM(...]
where the time goes in v9:
time: 16.3 us; the launch traced here: 16.1 us
  Pallas kernels  15.4 us (94%)
  local copies, waits for them, and re-layouts  0.71 us (4%)
    pallas_call x1, Pallas kernels, shards(): pl.pallas_call(functools.partial(body, C, T, rows), out_shape=pltpu.VMEM(...  15.4 us
    unnamed x1, local copies, waits for them, and re-layouts  0.71 us

profile of v9, /device:TPU:0, one launch (start us, length us, event | category | flops | bytes accessed | tf_op | source)
XLA Modules:
  0.0 16.1 jit_solution(16927943001236058917)
XLA Ops:
  0.0 15.4 %shard_map.46 = f32[16,16,256]{2,1,0:T(8,128)S(1)} custom-call(f32[32]{0:T(128)} %taps_hbm.1, s32[1,16]{1,0:T(1,128)} %pair_hbm.1, s32[2]{0:T(128)} %blocks_hbm.1, bf16[16,4096]{1,0:T(8,128)(2,1)} %rec_hbm.1), custom_call_target="tpu_custom_call" | custom-call | flops 600000000 | bytes 1000000 | tf_op jit(solution)/shard_map/pallas_call | solution.py:390
  15.4 0.7 %copy.6 = f32[2,8,16,256]{3,2,1,0:T(8,128)} copy(f32[2,8,16,256]{3,2,1,0:T(8,128)S(1)} %bitcast.1) | data formatting | bytes 524288

commit v10 on v9

--- a/solution.py
+++ b/solution.py
@@ -16,6 +16,7 @@
 FINE = 16
 SPILL = TAPS // 4
 FULL = 15
+NOTE = 16
 
 
 def body(C, T, rows, taps_hbm, pair_hbm, blocks_hbm, rec_hbm, out_ref,
@@ -152,7 +153,7 @@
         q, e = encode(filtered)
         note = jnp.where(lane == SPILL, e.astype(i32), jnp.where(lane == SPILL + 1, pick, q[:, samples:])).astype(i16)
         q = q[:, :samples].astype(i16)
-        own[t] = jnp.concatenate([q, note], axis=1)
+        own[t] = q
         halves[0] = jnp.concatenate([q[:, :part], note], axis=1)
         halves[1] = jnp.concatenate([q[:, part:], note], axis=1)
         plane[me] = halves[side]
@@ -188,7 +189,10 @@
         s.start()
 
     def combine(slot):
-        return scaled(plain(own[slot])) + scaled(permuted(pick, plain(partner[slot])))
+        note = plain(part_s[2 * slot + side][:, part:])
+        mine, theirs = (jnp.concatenate([plain(buf[slot]), pltpu.roll(note, LANES - NOTE * g, 1)], axis=1)
+                        for g, buf in ((1, own), (2, partner)))
+        return scaled(mine) + scaled(permuted(pick, theirs))
 
     with jax.named_scope("relay_first"):
         relay(0)
@@ -225,7 +229,10 @@
             q = jnp.round(mine * jnp.exp2(first - top - 1.0) + theirs * jnp.exp2(second - top - 1.0))
             last = jnp.where(lane[:VS] == SPILL, top, q[:, part:])
             picked.append(jnp.concatenate([q[:, :part], last], axis=1))
-        x = jnp.concatenate(picked, axis=0).astype(i32).astype(i16)
+        x = jnp.concatenate(picked, axis=0)
+        notes = [pltpu.roll(plain(plane[at][:, part:]), NOTE * g, 1) for g, at in ((1, me), (2, at_chan(half)))]
+        last = jnp.where(lane < NOTE, x[:, part:], jnp.where(lane < 2 * NOTE, *notes))
+        x = jnp.concatenate([x[:, :part], last], axis=1).astype(i32).astype(i16)
         mine_at = 2 * t + side
         part_s[mine_at] = x
 
@@ -286,8 +293,7 @@
         mate_copy.wait_recv()
         near_half, far_half = plain(plane[at_chan(half)]), plain(mate_rest[...])
         mate = jnp.concatenate([jnp.where(side == 0, near_half[:, :part], far_half[:, :part]),
-                                jnp.where(side == 0, far_half[:, :part], near_half[:, :part]),
-                                near_half[:, part:]], axis=1)
+                                jnp.where(side == 0, far_half[:, :part], near_half[:, :part])], axis=1)
         partner[t] = mate.astype(i32).astype(i16)
 
     def whiten_own():
@@ -314,27 +320,15 @@
         for i, x in enumerate(whiten(assemble(blocks))):
             src[i] = x
 
-    @pl.when(side == 0)
-    def _():
-        with jax.named_scope("wait_both"):
-            arrived(partner, T - 1, partner_r)
-            arrived(part_s, T, twin_r)
-        with jax.named_scope("prepare_both"):
-            whiten_own()
-            whiten_sources()
-            turn_own()
-
-    @pl.when(side == 1)
-    def _():
-        with jax.named_scope("wait_partner"):
-            arrived(partner, T - 1, partner_r)
-        with jax.named_scope("prepare_own"):
-            whiten_own()
-            turn_own()
-        with jax.named_scope("wait_twin"):
-            arrived(part_s, T, twin_r)
-        with jax.named_scope("prepare_sources"):
-            whiten_sources()
+    with jax.named_scope("wait_partner"):
+        arrived(partner, T - 1, partner_r)
+    with jax.named_scope("prepare_own"):
+        whiten_own()
+        turn_own()
+    with jax.named_scope("wait_twin"):
+        arrived(part_s, T, twin_r)
+    with jax.named_scope("prepare_sources"):
+        whiten_sources()
 
     with jax.named_scope("correlate"):
         z = None
@@ -401,8 +395,8 @@
             pltpu.VMEM((2, rows, samples // 2 + LANES), i16),
             pltpu.VMEM((C, rows, samples // 2 + LANES), i16),
             pltpu.VMEM((rows, samples // 2 + LANES), i16),
-            pltpu.VMEM((T, rows, samples + LANES), i16),
-            pltpu.VMEM((T, rows, samples + LANES), i16),
+            pltpu.VMEM((T, rows, samples), i16),
+            pltpu.VMEM((T, rows, samples), i16),
             pltpu.VMEM((2 * T, rows, samples // 2 + LANES), i16),
             pltpu.VMEM((T, rows, samples), bf16),
             pltpu.VMEM((rows, T * samples + LAGS + LANES), bf16),

time: 16.3 us -> 16.1 us (0.988)
  Pallas kernels: 15.4 us -> 15.1 us
    pallas_call x1, Pallas kernels: 15.4 us -> 15.1 us  [shards(): pl.pallas_call(functools.partial(body, C, T, rows), out_shape=pltpu.VMEM(...]
where the time goes in v10:
time: 16.1 us; the launch traced here: 15.8 us
  Pallas kernels  15.1 us (94%)
  local copies, waits for them, and re-layouts  0.71 us (4%)
    pallas_call x1, Pallas kernels, shards(): pl.pallas_call(functools.partial(body, C, T, rows), out_shape=pltpu.VMEM(...  15.1 us
    unnamed x1, local copies, waits for them, and re-layouts  0.71 us

profile of v10, /device:TPU:0, one launch (start us, length us, event | category | flops | bytes accessed | tf_op | source)
XLA Modules:
  0.0 15.8 jit_solution(13834016680400532768)
XLA Ops:
  0.0 15.1 %shard_map.46 = f32[16,16,256]{2,1,0:T(8,128)S(1)} custom-call(f32[32]{0:T(128)} %taps_hbm.1, s32[1,16]{1,0:T(1,128)} %pair_hbm.1, s32[2]{0:T(128)} %blocks_hbm.1, bf16[16,4096]{1,0:T(8,128)(2,1)} %rec_hbm.1), custom_call_target="tpu_custom_call" | custom-call | flops 600000000 | bytes 1000000 | tf_op jit(solution)/shard_map/pallas_call | solution.py:384
  15.1 0.7 %copy.6 = f32[2,8,16,256]{3,2,1,0:T(8,128)} copy(f32[2,8,16,256]{3,2,1,0:T(8,128)S(1)} %bitcast.1) | data formatting | bytes 524288

commit v11 on v10

--- a/solution.py
+++ b/solution.py
@@ -194,18 +194,19 @@
                         for g, buf in ((1, own), (2, partner)))
         return scaled(mine) + scaled(permuted(pick, theirs))
 
-    with jax.named_scope("relay_first"):
-        relay(0)
+    @pl.when(t == 0)
+    def _():
+        with jax.named_scope("relay_all"):
+            for k in (1, 0, *range(2, T - 1)) if T > 2 else range(T - 1):
+                relay(k)
+
+    @pl.when(t > 0)
+    def _():
+        with jax.named_scope("relay_first"):
+            relay(0)
 
     with jax.named_scope("wait_plane"):
         arrived(plane, C - 1, plane_r)
-
-    early = range(1, min(2, T - 1))
-    with jax.named_scope("relay_early"):
-        @pl.when(low)
-        def _():
-            for k in early:
-                relay(k)
 
     with jax.named_scope("pick"):
         picked = []
@@ -247,12 +248,10 @@
             s.start()
 
     with jax.named_scope("relay"):
-        @pl.when(jnp.logical_not(low))
+        @pl.when(t > 0)
         def _():
-            for k in early:
+            for k in range(1, T - 1):
                 relay(k)
-        for k in range(early.stop, T - 1):
-            relay(k)
 
     lag0 = t * lag_dev
     wide = samples + LANES

time: 16.1 us -> 15.8 us (0.981)
    pallas_call x1, Pallas kernels: 15.1 us -> 15 us  [shards(): pl.pallas_call(functools.partial(body, C, T, rows), out_shape=pltpu.VMEM(...]
where the time goes in v11:
time: 15.8 us; the launch traced here: 15.7 us
  Pallas kernels  15 us (95%)
  local copies, waits for them, and re-layouts  0.71 us (4%)
    pallas_call x1, Pallas kernels, shards(): pl.pallas_call(functools.partial(body, C, T, rows), out_shape=pltpu.VMEM(...  15 us
    unnamed x1, local copies, waits for them, and re-layouts  0.71 us

profile of v11, /device:TPU:0, one launch (start us, length us, event | category | flops | bytes accessed | tf_op | source)
XLA Modules:
  0.0 15.7 jit_solution(13829805824593741234)
XLA Ops:
  0.0 15.0 %shard_map.46 = f32[16,16,256]{2,1,0:T(8,128)S(1)} custom-call(f32[32]{0:T(128)} %taps_hbm.1, s32[1,16]{1,0:T(1,128)} %pair_hbm.1, s32[2]{0:T(128)} %blocks_hbm.1, bf16[16,4096]{1,0:T(8,128)(2,1)} %rec_hbm.1), custom_call_target="tpu_custom_call" | custom-call | flops 600000000 | bytes 1000000 | tf_op jit(solution)/shard_map/pallas_call | solution.py:383
  15.0 0.7 %copy.6 = f32[2,8,16,256]{3,2,1,0:T(8,128)} copy(f32[2,8,16,256]{3,2,1,0:T(8,128)S(1)} %bitcast.1) | data formatting | bytes 524288

commit v12 on v11

--- a/solution.py
+++ b/solution.py
@@ -21,7 +21,7 @@
 
 def body(C, T, rows, taps_hbm, pair_hbm, blocks_hbm, rec_hbm, out_ref,
          taps_ref, pair_ref, blocks_ref, rec_ref, local_s,
-         halves, plane, mate_rest, own, partner, part_s, src, wp, wall,
+         halves, plane, mate_rest, own, partner, gathered, part_s, src, wp, wall,
          plane_s, plane_r, own_s, own_r, mate_r, partner_s, partner_r,
          body_r, twin_s, twin_r):
     me = lax.axis_index("chan")
@@ -190,9 +190,9 @@
 
     def combine(slot):
         note = plain(part_s[2 * slot + side][:, part:])
-        mine, theirs = (jnp.concatenate([plain(buf[slot]), pltpu.roll(note, LANES - NOTE * g, 1)], axis=1)
-                        for g, buf in ((1, own), (2, partner)))
-        return scaled(mine) + scaled(permuted(pick, theirs))
+        mine = jnp.concatenate([plain(own[slot]), pltpu.roll(note, LANES - NOTE, 1)], axis=1)
+        there = permuted(pick, pltpu.roll(note, LANES - 2 * NOTE, 1))
+        return scaled(mine) + scaled(jnp.concatenate([gathered[slot], there], axis=1))
 
     @pl.when(t == 0)
     def _():
@@ -285,15 +285,21 @@
         scale = lax.rsqrt(jnp.sum(acc, axis=1, keepdims=True) / window + 1e-6)
         return [(x * scale).astype(bf16) for x in blocks]
 
-    with jax.named_scope("hand_to_twin"):
-        for k in range(T - 1):
-            hand_to_twin(k)
     with jax.named_scope("own_block"):
         mate_copy.wait_recv()
         near_half, far_half = plain(plane[at_chan(half)]), plain(mate_rest[...])
         mate = jnp.concatenate([jnp.where(side == 0, near_half[:, :part], far_half[:, :part]),
                                 jnp.where(side == 0, far_half[:, :part], near_half[:, :part])], axis=1)
         partner[t] = mate.astype(i32).astype(i16)
+
+    with jax.named_scope("wait_partner"):
+        arrived(partner, T - 1, partner_r)
+    with jax.named_scope("gather"):
+        for i in range(T):
+            gathered[i] = permuted(pick, plain(partner[i]))
+    with jax.named_scope("hand_to_twin"):
+        for k in range(T - 1):
+            hand_to_twin(k)
 
     def whiten_own():
         white = whiten(assemble([combine(i) for i in range(T)]))
@@ -319,8 +325,6 @@
         for i, x in enumerate(whiten(assemble(blocks))):
             src[i] = x
 
-    with jax.named_scope("wait_partner"):
-        arrived(partner, T - 1, partner_r)
     with jax.named_scope("prepare_own"):
         whiten_own()
         turn_own()
@@ -396,6 +400,7 @@
             pltpu.VMEM((rows, samples // 2 + LANES), i16),
             pltpu.VMEM((T, rows, samples), i16),
             pltpu.VMEM((T, rows, samples), i16),
+            pltpu.VMEM((T, rows, samples), f32),
             pltpu.VMEM((2 * T, rows, samples // 2 + LANES), i16),
             pltpu.VMEM((T, rows, samples), bf16),
             pltpu.VMEM((rows, T * samples + LAGS + LANES), bf16),

time: 15.8 us -> 15.8 us (level)
  no operation moved by 1% of the time
where the time goes in v12:
time: 15.8 us; the launch traced here: 15.7 us
  Pallas kernels  15 us (95%)
  local copies, waits for them, and re-layouts  0.71 us (4%)
    pallas_call x1, Pallas kernels, shards(): pl.pallas_call(functools.partial(body, C, T, rows), out_shape=pltpu.VMEM(...  15 us
    unnamed x1, local copies, waits for them, and re-layouts  0.71 us

profile of v12, /device:TPU:0, one launch (start us, length us, event | category | flops | bytes accessed | tf_op | source)
XLA Modules:
  0.0 15.7 jit_solution(4603999043190019119)
XLA Ops:
  0.0 15.0 %shard_map.46 = f32[16,16,256]{2,1,0:T(8,128)S(1)} custom-call(f32[32]{0:T(128)} %taps_hbm.1, s32[1,16]{1,0:T(1,128)} %pair_hbm.1, s32[2]{0:T(128)} %blocks_hbm.1, bf16[16,4096]{1,0:T(8,128)(2,1)} %rec_hbm.1), custom_call_target="tpu_custom_call" | custom-call | flops 600000000 | bytes 1000000 | tf_op jit(solution)/shard_map/pallas_call | solution.py:387
  15.0 0.7 %copy.6 = f32[2,8,16,256]{3,2,1,0:T(8,128)} copy(f32[2,8,16,256]{3,2,1,0:T(8,128)S(1)} %bitcast.1) | data formatting | bytes 524288

commit v13 on v12

--- a/solution.py
+++ b/solution.py
@@ -200,11 +200,6 @@
             for k in (1, 0, *range(2, T - 1)) if T > 2 else range(T - 1):
                 relay(k)
 
-    @pl.when(t > 0)
-    def _():
-        with jax.named_scope("relay_first"):
-            relay(0)
-
     with jax.named_scope("wait_plane"):
         arrived(plane, C - 1, plane_r)
 
@@ -250,7 +245,7 @@
     with jax.named_scope("relay"):
         @pl.when(t > 0)
         def _():
-            for k in range(1, T - 1):
+            for k in range(T - 1):
                 relay(k)
 
     lag0 = t * lag_dev

time: 15.8 us -> 15.8 us (level)
  Pallas kernels: 15 us -> 14.8 us
where the time goes in v13:
time: 15.8 us; the launch traced here: 15.6 us
  Pallas kernels  14.8 us (94%)
  local copies, waits for them, and re-layouts  0.71 us (4%)
    pallas_call x1, Pallas kernels, shards(): pl.pallas_call(functools.partial(body, C, T, rows), out_shape=pltpu.VMEM(...  14.8 us
    unnamed x1, local copies, waits for them, and re-layouts  0.71 us

profile of v13, /device:TPU:0, one launch (start us, length us, event | category | flops | bytes accessed | tf_op | source)
XLA Modules:
  0.0 15.6 jit_solution(11729366139002977370)
XLA Ops:
  0.0 14.8 %shard_map.46 = f32[16,16,256]{2,1,0:T(8,128)S(1)} custom-call(f32[32]{0:T(128)} %taps_hbm.1, s32[1,16]{1,0:T(1,128)} %pair_hbm.1, s32[2]{0:T(128)} %blocks_hbm.1, bf16[16,4096]{1,0:T(8,128)(2,1)} %rec_hbm.1), custom_call_target="tpu_custom_call" | custom-call | flops 600000000 | bytes 1000000 | tf_op jit(solution)/shard_map/pallas_call | solution.py:382
  14.8 0.7 %copy.6 = f32[2,8,16,256]{3,2,1,0:T(8,128)} copy(f32[2,8,16,256]{3,2,1,0:T(8,128)S(1)} %bitcast.1) | data formatting | bytes 524288

commit v14 on v12

--- a/solution.py
+++ b/solution.py
@@ -22,7 +22,7 @@
 def body(C, T, rows, taps_hbm, pair_hbm, blocks_hbm, rec_hbm, out_ref,
          taps_ref, pair_ref, blocks_ref, rec_ref, local_s,
          halves, plane, mate_rest, own, partner, gathered, part_s, src, wp, wall,
-         plane_s, plane_r, own_s, own_r, mate_r, partner_s, partner_r,
+         plane_s, plane_r, own_s, own_r, mate_s, mate_r, partner_s, partner_r,
          body_r, twin_s, twin_r):
     me = lax.axis_index("chan")
     t = lax.axis_index("tm")
@@ -163,7 +163,8 @@
 
     with jax.named_scope("send_filtered"):
         others = [d for d in range(1, C) if d != half]
-        mate_copy = remote(halves.at[lax.rem(side + half + 1, 2)], mate_rest, plane_s, mate_r, {"chan": at_chan(half)})
+        mate_copy = remote(halves.at[lax.rem(side + half + 1, 2), :, pl.ds(0, part)], mate_rest, mate_s, mate_r,
+                           {"chan": at_chan(half)})
         others = [half] + others
         sends = [remote(halves.at[lax.rem(side + d, 2)], plane.at[me], plane_s, plane_r,
                          {"chan": at_chan(d)}) for d in others]
@@ -287,9 +288,9 @@
 
     with jax.named_scope("own_block"):
         mate_copy.wait_recv()
-        near_half, far_half = plain(plane[at_chan(half)]), plain(mate_rest[...])
-        mate = jnp.concatenate([jnp.where(side == 0, near_half[:, :part], far_half[:, :part]),
-                                jnp.where(side == 0, far_half[:, :part], near_half[:, :part])], axis=1)
+        near_half, far_half = plain(plane[at_chan(half)])[:, :part], plain(mate_rest[...])
+        mate = jnp.concatenate([jnp.where(side == 0, near_half, far_half),
+                                jnp.where(side == 0, far_half, near_half)], axis=1)
         partner[t] = mate.astype(i32).astype(i16)
 
     with jax.named_scope("wait_partner"):
@@ -369,9 +370,10 @@
                     out_ref[lo_s + s, :, LANES * p:LANES * p + span_out] = o[:, :span_out]
 
     with jax.named_scope("wait_sends"):
-        for buf, count, sem in ((plane, C, plane_s), (own, T - 1, own_s), (partner, T - 1, partner_s),
+        for buf, count, sem in ((plane, C - 1, plane_s), (own, T - 1, own_s), (partner, T - 1, partner_s),
                                 (part_s, 2 * T - 1, twin_s)):
             gone(buf, count, sem)
+        mate_copy.wait_send()
 
 
 def shards(records, pair_rows, fir_taps, source_blocks):
@@ -397,7 +399,7 @@
             dma((4,)),
             pltpu.VMEM((2, rows, samples // 2 + LANES), i16),
             pltpu.VMEM((C, rows, samples // 2 + LANES), i16),
-            pltpu.VMEM((rows, samples // 2 + LANES), i16),
+            pltpu.VMEM((rows, samples // 2), i16),
             pltpu.VMEM((T, rows, samples), i16),
             pltpu.VMEM((T, rows, samples), i16),
             pltpu.VMEM((T, rows, samples), f32),
@@ -405,7 +407,7 @@
             pltpu.VMEM((T, rows, samples), bf16),
             pltpu.VMEM((rows, T * samples + LAGS + LANES), bf16),
             pltpu.VMEM((min(LAGS // T, LANES) // FINE * rows, T * samples + LANES * max(1, LAGS // T // LANES)), bf16),
-            dma, dma, dma, dma((T - 1,)), dma, dma, dma, dma((T - 1,)), dma, dma,
+            dma, dma, dma, dma((T - 1,)), dma, dma, dma, dma, dma((T - 1,)), dma, dma,
         ],
         compiler_params=pltpu.CompilerParams(
             collective_id=0, has_side_effects=True,

time: 15.8 us -> 15.9 us (level)
  no operation moved by 1% of the time
where the time goes in v14:
time: 15.9 us; the launch traced here: 15.7 us
  Pallas kernels  15 us (94%)
  local copies, waits for them, and re-layouts  0.71 us (4%)
    pallas_call x1, Pallas kernels, shards(): pl.pallas_call(functools.partial(body, C, T, rows), out_shape=pltpu.VMEM(...  15 us
    unnamed x1, local copies, waits for them, and re-layouts  0.71 us

profile of v14, /device:TPU:0, one launch (start us, length us, event | category | flops | bytes accessed | tf_op | source)
XLA Modules:
  0.0 15.7 jit_solution(6759838164108145977)
XLA Ops:
  0.0 15.0 %shard_map.46 = f32[16,16,256]{2,1,0:T(8,128)S(1)} custom-call(f32[32]{0:T(128)} %taps_hbm.1, s32[1,16]{1,0:T(1,128)} %pair_hbm.1, s32[2]{0:T(128)} %blocks_hbm.1, bf16[16,4096]{1,0:T(8,128)(2,1)} %rec_hbm.1), custom_call_target="tpu_custom_call" | custom-call | flops 600000000 | bytes 1000000 | tf_op jit(solution)/shard_map/pallas_call | solution.py:389
  15.0 0.7 %copy.6 = f32[2,8,16,256]{3,2,1,0:T(8,128)} copy(f32[2,8,16,256]{3,2,1,0:T(8,128)S(1)} %bitcast.1) | data formatting | bytes 524288
